TPU v7x, 256 devices: a whole 4x4x8 slice. The times are simulated.
256 devices in a mesh: dp: 16 (over x, y_hi, core), tensor: 16 (over y_lo, z).
Axes of the slice: x: 4, y: 4 (y_hi: 2, y_lo: 2; y = y_hi * 2 + y_lo), z: 8, core: 2. Of those that a mesh axis runs over, the one named last changes fastest.
Arguments:
- learner_layer_inputs: bfloat16 [49152, 16384], P('dp', 'tensor'), may hold values from -6 to 6
- trainer_lookup_content_adjoint: bfloat16 [49152, 2048], P('dp', 'tensor'), may hold values from -6 to 6
- frozen_weight: bfloat16 [16384, 2048], P('tensor'), may hold values from -0.046875 to 0.046875
- shrink_matrices: float32 [16384, 128], P('tensor'), may hold values from -0.046875 to 0.046875
- expand_matrices: float32 [64, 2048], P(None, 'tensor'), may hold values from -0.3 to 0.3
- decode_hidden_states: bfloat16 [4096, 16384], P('dp', 'tensor'), may hold values from -6 to 6
- rms_norm_gain: float32 [16384], P('tensor'), may hold values from 0.1 to 1.9
Outputs:
- new_keys_values: float32 [2048, 4096], P('tensor', 'dp')
All inputs are finite; a program needn't handle non-finite values.
Results may differ from a plain program's by a relative error of at most 0.0041.
Values sent between devices are 32-bit elements; how exact they have to be, the bound alone decides.
A program may use at most 64 MiB of HBM per device.

v0:
```python
import jax
import jax.numpy as jnp
from jax import lax
from jax.sharding import PartitionSpec as P

EMBED_DIMENSION = 16384


delta_multiplier = 2.0
learning_rate = 4.0
clip_limit = 1.0


def token_axis_summation(left, right):
    return lax.dot_general(
        left, right, (((0,), (0,)), ((), ())), preferred_element_type=jnp.float32
    )


def shards(
    learner_layer_inputs,
    trainer_lookup_content_adjoint,
    frozen_weight,
    shrink_matrices,
    expand_matrices,
    decode_hidden_states,
    rms_norm_gain,
):
    width_all = frozen_weight.shape[1]
    half_width = width_all // 2
    adapter_rank_width = shrink_matrices.shape[1] // 2
    column_span = expand_matrices.shape[1]
    column_start = lax.axis_index("tensor") * column_span
    key_block = column_start < half_width
    down_factor_cast = shrink_matrices.astype(jnp.bfloat16)
    up_factor_cast = expand_matrices.astype(jnp.bfloat16)
    proj_part = jnp.dot(learner_layer_inputs, down_factor_cast, preferred_element_type=jnp.float32)
    backing = lax.dot_general(
        trainer_lookup_content_adjoint,
        up_factor_cast,
        (((1,), (1,)), ((), ())),
        preferred_element_type=jnp.float32,
    )
    blank = jnp.zeros_like(backing)
    back_part = jnp.where(
        key_block,
        jnp.concatenate([backing, blank], axis=1),
        jnp.concatenate([blank, backing], axis=1),
    )
    proj_full, back_full = lax.psum((proj_part, back_part), "tensor")
    mapped_result = (delta_multiplier * proj_full).astype(jnp.bfloat16)
    gradient_held = (delta_multiplier * back_full).astype(jnp.bfloat16)
    local_projection = jnp.where(
        key_block, mapped_result[:, :adapter_rank_width], mapped_result[:, adapter_rank_width:]
    )
    down_gradient = token_axis_summation(learner_layer_inputs, gradient_held)
    expand_derivative = token_axis_summation(local_projection, trainer_lookup_content_adjoint)
    down_gradient, expand_derivative = lax.psum((down_gradient, expand_derivative), "dp")
    local_total = jnp.sum(down_gradient * down_gradient) + jnp.sum(
        expand_derivative * expand_derivative
    )
    total = lax.psum(local_total, "tensor")
    factor_matrix = jnp.minimum(1.0, clip_limit / (jnp.sqrt(total) + 1e-06))
    revised_shrink_matrix = shrink_matrices - learning_rate * factor_matrix * down_gradient
    revised_expand_matrix = expand_matrices - learning_rate * factor_matrix * expand_derivative
    full_up = lax.all_gather(revised_expand_matrix, "tensor", axis=1, tiled=True)
    attention_lookup_thin = jnp.dot(
        revised_shrink_matrix[:, :adapter_rank_width],
        full_up[:, :half_width],
        precision=lax.Precision.HIGHEST,
    )
    content_thin_product = jnp.dot(
        revised_shrink_matrix[:, adapter_rank_width:],
        full_up[:, half_width:],
        precision=lax.Precision.HIGHEST,
    )
    merged_weight = (
        frozen_weight.astype(jnp.float32)
        + delta_multiplier * jnp.concatenate([attention_lookup_thin, content_thin_product], axis=1)
    ).astype(jnp.bfloat16)
    widened = decode_hidden_states.astype(jnp.float32)
    row_total = lax.psum(jnp.sum(widened * widened, axis=1), "tensor")
    scaling = lax.rsqrt(row_total / EMBED_DIMENSION + 1e-05)
    normed = (widened * scaling[:, None] * rms_norm_gain[None, :]).astype(jnp.bfloat16)
    return lax.psum_scatter(
        lax.dot_general(
            merged_weight, normed, (((0,), (1,)), ((), ())), preferred_element_type=jnp.float32
        ),
        "tensor",
        scatter_dimension=0,
        tiled=True,
    )


def solution(mesh):
    placed = (
        P("dp", "tensor"),
        P("dp", "tensor"),
        P("tensor", None),
        P("tensor", None),
        P(None, "tensor"),
        P("dp", "tensor"),
        P("tensor"),
    )
    return jax.shard_map(
        shards, mesh=mesh, in_specs=placed, out_specs=P("tensor", "dp"), check_vma=False
    )
```

profile of v0, /device:TPU:6, one launch (start us, length us, event | category | flops | bytes accessed | tf_op | source)
XLA Modules:
  0.0 472.1 jit_solution(15392840804945207122)
XLA Ops:
  6.5 1.1 copy-done
  7.7 1.1 fusion.22
  8.8 1.3 pad_select_fusion
  10.1 6.2 %fusion.20 = f32[3072,128]{0,1:T(8,128)} fusion(bf16[3072,1024]{1,0:T(8,128)(2,1)} %param.7, f32[1024,128]{1,0:T(8,128)S(1)} %copy-done.1), kind=kOutput, calls=%fused_computation.28 | convolution fusion | flops 805437440 | bytes 8388608 | tf_op jit(solution)/shard_map/dot_general | solution.py:37
  16.3 0.0 all-reduce.9.cloned.1.call-update
  16.3 0.0 all-reduce.7.cloned.1.call-start
  16.4 0.2 fusion.4
  16.6 151.6 %all-reduce.9.cloned.1.call-done = (f32[3072,128]{0,1:T(8,128)}, f32[3072,128]{0,1:T(8,128)}) async-done(((f32[3072,128]{0,1:T(8,128)}, f32[3072,128]{0,1:T(8,128)}), (f32[3072,128]{0,1:T(8,128)}, f32[3072,128]{0,1:T(8,128)})) %all-reduce.9.cloned.1.call-update) | async-done | bytes 3145744 | tf_op jit(solution)/shard_map/psum | solution.py:50
  168.2 5.2 %convolution_bitcast_fusion = f32[1024,128]{0,1:T(8,128)} fusion(bf16[3072,1024]{1,0:T(8,128)(2,1)} %param.7, f32[3072,128]{0,1:T(8,128)} %get-tuple-element.8), kind=kOutput, calls=%fused_computation.9 | convolution fusion | flops 806092800 | bytes 8388608 | tf_op jit(solution)/shard_map/dot_general | solution.py:15
  173.4 0.0 reduce-scatter.2.cloned.1.call-start
  173.4 0.1 multiply_convert_fusion
  173.5 0.3 fusion.11
  173.8 55.7 %psum.45 = f32[64,128]{1,0:T(8,128)S(1)} all-reduce(f32[64,128]{1,0:T(8,128)S(1)} %fusion.11), channel_id=1, replica_groups=mesh['dp'=16,'tensor'=16] {'dp'}, use_global_device_ids=true, to_apply=%region_4.5 | all-reduce | flops 8192 | bytes 65536 | tf_op jit(solution)/shard_map/psum | solution.py:58
  229.5 0.6 multiply_reduce_fusion.1
  230.2 77.4 %all-reduce.7.cloned.1.call-done = f32[1024,128]{0,1:T(8,128)} async-done(((f32[1024,128]{0,1:T(8,128)}), f32[1024,128]{0,1:T(8,128)}) %all-reduce.7.cloned.1.call-update) | async-done | bytes 524304 | tf_op jit(solution)/shard_map/psum | solution.py:58
  307.5 1.8 multiply_reduce_fusion
  310.6 0.2 copy.9
  310.8 35.1 %all-reduce.2 = (f32[]{:T(128)}, f32[256]{0:T(256)S(1)}) all-reduce(f32[]{:T(128)S(6)} %add.33, f32[256]{0:T(256)S(1)} %fusion.4), channel_id=1, replica_groups=mesh['dp'=16,'tensor'=16] {'tensor'}, use_global_device_ids=true, to_apply=%region_6.7 | all-reduce | flops 257 | bytes 2056 | tf_op jit(solution)/shard_map/psum | solution.py:62
  346.7 33.0 %all_gather.3 = f32[64,2048]{1,0:T(8,128)S(1)} all-gather(f32[64,128]{1,0:T(8,128)S(1)} %multiply_subtract_fusion.1), channel_id=1, replica_groups=mesh['dp'=16,'tensor'=16] {'tensor'}, dimensions={1}, use_global_device_ids=true | all-gather | bytes 557056 | tf_op jit(solution)/shard_map/all_gather | solution.py:66
  379.7 1.1 multiply_subtract_fusion
  380.8 3.5 fusion.14
  384.3 3.5 fusion.17
  387.9 3.7 fusion.2
  391.6 74.0 %reduce-scatter.2.cloned.1.call-done = f32[128,256]{1,0:T(8,128)} async-done(((f32[2048,256]{1,0:T(8,128)}), f32[128,256]{1,0:T(8,128)}) %reduce-scatter.2.cloned.1.call-update) | async-done | bytes 131088 | tf_op jit(solution)/shard_map/reduce_scatter | solution.py:85
  (20 shorter events, 0.1 us)
Async XLA Ops:
  6.5 1.1 copy-start
  6.5 3.6 copy-start.1
  6.5 161.6 %all-reduce.9.cloned.1.call-start = ((), (), s32[]{:S(2)}) async-start(), calls=%async_computation.3 | async-start | bytes 6291456 | tf_op jit(solution)/shard_map/psum | solution.py:50
  10.1 6.3 %copy-start.3 = (bf16[256,1024]{1,0:T(8,128)(2,1)S(1)}, bf16[256,1024]{1,0:T(8,128)(2,1)}, u32[]{:S(2)}) copy-start(bf16[256,1024]{1,0:T(8,128)(2,1)} %param.12) | copy-start | bytes 1572868
  16.3 291.2 %all-reduce.7.cloned.1.call-start = ((), (), s32[]{:S(2)}) async-start(), calls=%async_computation.1 | async-start | bytes 1048576 | tf_op jit(solution)/shard_map/psum | solution.py:58
  168.2 5.2 %copy-start.2 = (f32[3072,128]{0,1:T(8,128)S(1)}, f32[3072,128]{0,1:T(8,128)}, u32[]{:S(2)}) copy-start(f32[3072,128]{0,1:T(8,128)} %get-tuple-element.7) | copy-start | bytes 4718596
  173.3 173.3 %copy-start.5 = (f32[64,128]{1,0:T(8,128)S(1)}, f32[64,128]{1,0:T(8,128)}, u32[]{:S(2)}) copy-start(f32[64,128]{1,0:T(8,128)} %param.11) | copy-start | bytes 98308
  173.4 292.2 %reduce-scatter.2.cloned.1.call-start = ((), (), s32[]{:S(2)}) async-start(), calls=%async_computation.2 | async-start | bytes 2228224 | tf_op jit(solution)/shard_map/reduce_scatter | solution.py:85
  380.8 7.1 %copy-start.4 = (bf16[256,1024]{1,0:T(8,128)(2,1)S(1)}, bf16[256,1024]{1,0:T(8,128)(2,1)}, u32[]{:S(2)}) copy-start(bf16[256,1024]{1,0:T(8,128)(2,1)} %param.12) | copy-start | bytes 1572868
  380.8 7.1 %copy-start.6 = (bf16[1024,2048]{1,0:T(8,128)(2,1)S(1)}, bf16[1024,2048]{1,0:T(8,128)(2,1)}, u32[]{:S(2)}) copy-start(bf16[1024,2048]{1,0:T(8,128)(2,1)} %param.9) | copy-start | bytes 12582916
  380.8 7.1 %copy-start.7 = (f32[1024]{0:T(1024)S(1)}, f32[1024]{0:T(1024)}, u32[]{:S(2)}) copy-start(f32[1024]{0:T(1024)} %param.13) | copy-start | bytes 12292
Sparse Core Ops, SparseCore 0:
  16.5 151.6 all-reduce.8
  173.5 134.0 all-reduce.6
  391.7 73.8 reduce-scatter.1
where the time goes:
time: 472 us
  waiting for transfers between devices  303 us (64%)
  blocking collectives  124 us (26%)
  matrix products  23.5 us (5%)
  between operations  15.3 us (3%)
  other arithmetic  5.13 us (1%)
    psum x1, waiting for transfers between devices, shards(): proj_full, back_full = lax.psum((proj_part, back_part), 'tensor')  152 us
    psum x1, waiting for transfers between devices, shards(): lax.psum((down_gradient, expand_derivative), 'dp')  77.4 us
    reduce_scatter x1, waiting for transfers between devices, shards(): lax.psum_scatter(lax.dot_general(merged_weight, normed, (((0,), (1,)), ((...  74 us
    psum x1, blocking collectives, shards(): lax.psum((down_gradient, expand_derivative), 'dp')  55.7 us
    psum x1, blocking collectives, shards(): total = lax.psum(local_total, 'tensor')  35.1 us
    all_gather x1, blocking collectives, shards(): lax.all_gather(revised_expand_matrix, 'tensor', axis=1, tiled=True)  33 us
  transfers between devices with their start and end apart: 3, of which 3 were waited for; matrix products, arithmetic and copies ran while one was open for 0% of the time, Pallas kernels for 0%

commit v1 on v0

v1 whole, which is shorter than its diff:
```python
import functools

import jax
import jax.numpy as jnp
from jax import lax
from jax.experimental import pallas as pl
from jax.experimental.pallas import tpu as pltpu
from jax.sharding import PartitionSpec as P

MESH = pl.DeviceIdType.MESH
F32 = jnp.float32
BF16 = jnp.bfloat16

EMBED_DIMENSION = 16384
delta_multiplier = 2.0
learning_rate = 4.0
clip_limit = 1.0

Z = 8
T = 16
E = 8
CH = 192
HALF = 1536


def rc(src, dst, ss, rs, dev):
    return pltpu.make_async_remote_copy(
        src_ref=src, dst_ref=dst, send_sem=ss, recv_sem=rs, device_id=dev, device_id_type=MESH
    )


def low_lanes(rows):
    return lax.broadcasted_iota(jnp.int32, (rows, 128), 1) < 64


def swap(v):
    return pltpu.roll(v, 64, 1)


def dot(a, b):
    return jnp.dot(a, b, preferred_element_type=F32)


def dot_nt(a, b):
    return lax.dot_general(a, b, (((1,), (1,)), ((), ())), preferred_element_type=F32)


def dot_tn(a, b):
    return lax.dot_general(a, b, (((0,), (0,)), ((), ())), preferred_element_type=F32)


def split(v):
    hi = v.astype(BF16)
    return hi, (v - hi.astype(F32)).astype(BF16)


class RingReduce:
    def __init__(self, own, buf, ss, rs, z, dev):
        self.own, self.buf, self.ss, self.rs, self.z, self.dev = own, buf, ss, rs, z, dev

    def chunk(self, d, far):
        return lax.rem(self.z + (far if d == 0 else Z - far), Z)

    def copy(self, d, h, s):
        first = 1 if d == h else 2
        if s == first:
            src = self.own(self.chunk(d, 5 - s), h)
        else:
            src = self.buf.at[d, s - 2, h]
        return rc(src, self.buf.at[d, s - 1, h], self.ss.at[d, h, s - 1], self.rs.at[d, h, s - 1], self.dev(d))

    def begin(self, first):
        for d in range(2):
            h = d if first == 1 else 1 - d
            self.copy(d, h, first).start()

    def step(self, s):
        for same in (True, False):
            if s == 1 and not same:
                continue
            for d in range(2):
                h = d if same else 1 - d
                self.copy(d, h, s).wait_recv()
                if s < 4:
                    self.buf[d, s - 1, h] += self.own(self.chunk(d, 4 - s), h)[...]
                    self.copy(d, h, s + 1).start()

    def result(self, h):
        return self.own(self.z, h)[...] + (self.buf[0, 3, h] + self.buf[1, 3, h])

    def drain(self):
        for d in range(2):
            for h in range(2):
                for s in range(1 if d == h else 2, 5):
                    self.copy(d, h, s).wait_send()


class RingGather:
    def __init__(self, arr, ss, rs, z, dev):
        self.arr, self.ss, self.rs, self.z, self.dev = arr, ss, rs, z, dev

    def copy(self, d, p, s):
        k = lax.rem(self.z + (Z - (s - 1) if d == 0 else s - 1), Z)
        ref = self.arr.at[k, p]
        return rc(ref, ref, self.ss.at[d, p, s - 1], self.rs.at[d, p, s - 1], self.dev(d))

    def begin(self):
        for p in range(2):
            for d in range(2):
                self.copy(d, p, 1).start()

    def step(self, s):
        for p in range(2):
            for d in range(2):
                last = 4 if d == p else 3
                if s <= last:
                    self.copy(d, p, s).wait_recv()
                    if s + 1 <= last:
                        self.copy(d, p, s + 1).start()

    def drain(self):
        for d in range(2):
            for p in range(2):
                for s in range(1, (4 if d == p else 3) + 1):
                    self.copy(d, p, s).wait_send()


def kernel(
    x_hbm, a_hbm, w_hbm, d_hbm, u_hbm, h_hbm, gain_hbm, o_ref,
    xv, av, wv, dv, uv, hv, gv, db, ub,
    bm, br, bag, pm, pt, py, pr, pag, om, oy, orr,
    gt, gc, gr, gf, gu, gur, guc, guf, rows, norms, normed, base,
    q0, q0r, q0a, qg, qgr, qga,
    ld, xs, s4, r4, y_s, y_r, t_s, t_r, z_s, z_r, e_s, e_r, c_s, c_r,
):
    dpi = lax.axis_index("dp")
    t = lax.axis_index("tensor")
    e, c = dpi // 2, lax.rem(dpi, 2)
    y, z = t // Z, lax.rem(t, Z)
    zdev = (dpi, y * Z + lax.rem(z + 1, Z)), (dpi, y * Z + lax.rem(z + Z - 1, Z))
    ydev = (dpi, (1 - y) * Z + z)
    cdev = (e * 2 + 1 - c, t)

    def ring(d):
        return zdev[d]

    def tdev(k):
        return (dpi, k)

    def edev(k):
        return (k * 2 + c, t)

    def order(j):
        far = 4 - (j + 1) // 2
        return lax.rem(z + (1 - 2 * lax.rem(j + 1, 2)) * far + Z, Z)

    def loop(n, body):
        def step(i, carry):
            body(i)
            return carry

        lax.fori_loop(0, n, step, 0)

    def local(src, dst, i):
        return pltpu.make_async_copy(src, dst, ld.at[i])

    l_u, l_a, l_d = local(u_hbm, uv, 0), local(a_hbm, av, 1), local(d_hbm, dv, 2)
    l_h, l_g, l_w = local(h_hbm, hv, 3), local(gain_hbm, gv, 4), local(w_hbm, wv, 5)

    def tok(k, second):
        return pl.ds(pl.multiple_of(k * CH + second * HALF, CH), CH)

    def xload(j, second):
        sl = tok(order(j), second)
        return pltpu.make_async_copy(x_hbm.at[sl], xv.at[sl], xs.at[j, second])

    l_u.start()
    l_a.start()
    l_d.start()

    @functools.partial(loop, Z)
    def _(j):
        xload(j, 0).start()
        xload(j, 1).start()

    l_h.start()
    l_g.start()
    l_w.start()

    barrier = pltpu.get_barrier_semaphore()

    def hello(dev):
        pl.semaphore_signal(barrier, inc=1, device_id=dev, device_id_type=MESH)

    hello(cdev)
    loop(T - 1, lambda i: hello(tdev(lax.rem(t + 1 + i, T))))
    loop(E - 1, lambda i: hello(edev(lax.rem(e + 1 + i, E))))

    l_u.wait()
    l_a.wait()
    ub[...] = uv[...].astype(BF16)
    blank = jnp.zeros((64, 128), BF16)

    @functools.partial(loop, Z)
    def _(k):
        u1 = jnp.concatenate([ub[...], blank], axis=0)
        u2 = jnp.concatenate([blank, ub[...]], axis=0)
        v = dot_nt(av[tok(k, 0), :], u1) + dot_nt(av[tok(k, 1), :], u2)
        bm[k] = v.reshape(2, CH // 2, 128)

    pl.semaphore_wait(barrier, T - 1 + E - 1 + 1)

    b_rs = RingReduce(lambda k, h: bm.at[k, h], br, s4.at[0], r4.at[0], z, ring)
    b_ag = RingGather(bag, s4.at[1], r4.at[1], z, ring)
    p_rs = RingReduce(lambda k, h: pm.at[k, h], pr, s4.at[2], r4.at[2], z, ring)
    p_ag = RingGather(pag, s4.at[3], r4.at[3], z, ring)
    o_rs = RingReduce(lambda k, h: om.at[y * Z + k, h], orr, s4.at[4], r4.at[4], z, ring)
    b_rs.begin(1)
    b_rs.begin(2)

    def p_y(j):
        k = order(j)
        return rc(pt.at[k], py.at[k], y_s.at[0, j], y_r.at[0, j], ydev)

    def o_y(j):
        k = order(j)
        return rc(om.at[(1 - y) * Z + k], oy.at[k], y_s.at[1, j], y_r.at[1, j], ydev)

    b_y = rc(bag.at[z, y], bag.at[z, y], y_s.at[2, 0], y_r.at[2, 0], ydev)
    b_y_in = rc(bag.at[z, 1 - y], bag.at[z, 1 - y], y_s.at[2, 0], y_r.at[2, 0], ydev)

    def p_add(j):
        p_y(j).wait_recv()
        k = order(j)
        pm[k] += py[k]

    def o_add(j):
        o_y(j).wait_recv()
        k = order(j)
        om[y * Z + k] += oy[k]

    l_d.wait()
    dd = dv[...]
    db[...] = jnp.where(y == 0, dd, swap(dd)).astype(BF16)

    @functools.partial(loop, Z)
    def _(j):
        k = order(j)
        xload(j, 0).wait()
        xload(j, 1).wait()
        pa = dot(xv[tok(k, 0), :], db[...])
        pb = dot(xv[tok(k, 1), :], db[...])
        low = low_lanes(CH)
        pm[k] = jnp.where(low, pa, swap(pb)).reshape(2, CH // 2, 128)
        pt[k] = jnp.where(low, swap(pa), pb).reshape(2, CH // 2, 128)

        @pl.when(j < 4)
        def _():
            p_y(j).start()

    def t_copy(n, src, dst, k):
        return rc(src, dst, t_s.at[n, k], t_r.at[n, t], tdev(k))

    def t_send(n, src, dst):
        loop(T - 1, lambda i: t_copy(n, src(lax.rem(t + 1 + i, T)), dst, lax.rem(t + 1 + i, T)).start())

    def t_recv(n, like, dst):
        def body(i):
            k = lax.rem(t + 1 + i, T)
            rc(like, dst.at[k], t_s.at[n, k], t_r.at[n, k], tdev(k)).wait_recv()

        loop(T - 1, body)

    def t_drain(n, src, dst):
        loop(T - 1, lambda i: t_copy(n, src(lax.rem(t + 1 + i, T)), dst, lax.rem(t + 1 + i, T)).wait_send())

    def z_copy(n, arr, i):
        k = lax.rem(z + 1 + i, Z)
        return rc(arr.at[z], arr.at[z], z_s.at[n, k], z_r.at[n, z], tdev(y * Z + k))

    def z_send(n, arr):
        loop(Z - 1, lambda i: z_copy(n, arr, i).start())

    def z_recv(n, arr):
        def body(i):
            k = lax.rem(z + 1 + i, Z)
            rc(arr.at[k], arr.at[k], z_s.at[n, k], z_r.at[n, k], tdev(y * Z + k)).wait_recv()

        loop(Z - 1, body)

    def e_copy(n, src, dst, k):
        return rc(src, dst, e_s.at[n, k], e_r.at[n, e], edev(k))

    def e_each(body):
        loop(E - 1, lambda i: body(lax.rem(e + 1 + i, E)))

    def pack(v, n):
        low = low_lanes(n)
        a, b = v[:n], v[n:]
        return jnp.where(low, a, swap(b)), jnp.where(low, swap(a), b)

    l_h.wait()
    l_g.wait()
    hf = hv[...].astype(F32)
    sq = jnp.sum(hf * hf, axis=1, keepdims=True)
    rows[t] = jnp.transpose(jnp.broadcast_to(sq, (256, 128)))[:8]
    t_send(0, lambda k: rows.at[t], rows.at[t])

    b_rs.step(1)
    p_add(0)
    p_rs.begin(1)
    b_rs.step(2)
    p_add(1)
    p_add(2)
    p_rs.begin(2)
    b_rs.step(3)
    p_rs.step(1)
    b_rs.step(4)
    for h in range(2):
        bag[z, y, h * 96 : (h + 1) * 96] = b_rs.result(h)
    b_y.start()
    loop(4, lambda j: p_y(j + 4).start())

    t_recv(0, rows.at[t], rows)
    mean = jnp.sum(rows[...], axis=0) / EMBED_DIMENSION
    scale = lax.rsqrt(mean + 1e-05)
    scale = jnp.transpose(jnp.broadcast_to(scale[:1], (128, 256)))
    for i in range(8):
        sl = slice(i * 128, (i + 1) * 128)
        normed[:, sl] = (hv[:, sl].astype(F32) * scale * gv[:, sl]).astype(BF16)

    b_y_in.wait_recv()
    b_ag.begin()

    l_w.wait()

    def out_pair(i):
        v = dot(normed[...], wv[:, pl.ds(pl.multiple_of(i * 256, 256), 256)])
        om[2 * i] = v[:, :128].reshape(2, 128, 128)
        om[2 * i + 1] = v[:, 128:].reshape(2, 128, 128)

    loop(4, lambda i: out_pair((1 - y) * 4 + i))
    loop(Z, lambda j: o_y(j).start())

    p_add(3)
    p_add(4)
    p_rs.step(2)

    def grad(k):
        kc, vc = bag[k, 0], bag[k, 1]
        low = low_lanes(CH)
        ba = jnp.where(low, kc, swap(vc)) * delta_multiplier
        bb = jnp.where(low, swap(kc), vc) * delta_multiplier
        v = dot_tn(ba.astype(BF16), xv[tok(k, 0), :]) + dot_tn(bb.astype(BF16), xv[tok(k, 1), :])
        return v.reshape(16, 8, 1024)

    gt[...] = grad(z)
    b_ag.step(1)
    loop(4, lambda i: out_pair(y * 4 + i))
    p_add(5)
    p_add(6)
    p_rs.step(3)
    loop(2, lambda i: gt.__setitem__(Ellipsis, gt[...] + grad(lax.rem(z + 1 + i * (Z - 2), Z))))
    b_ag.step(2)

    dhi, dlo = split(dv[...])
    qk, qv = pack(dot(normed[...], dhi) + dot(normed[...], dlo), 128)
    q0[0:8] = qk.reshape(8, 16, 128)
    q0[8:16] = qv.reshape(8, 16, 128)
    q0r[t] = q0[t]
    t_send(1, lambda k: q0.at[k], q0r.at[t])

    loop(2, lambda i: gt.__setitem__(Ellipsis, gt[...] + grad(lax.rem(z + 2 + i * (Z - 4), Z))))
    p_add(7)
    p_rs.step(4)
    for h in range(2):
        pag[z, h] = p_rs.result(h)
    b_ag.step(3)
    p_ag.begin()
    loop(2, lambda i: gt.__setitem__(Ellipsis, gt[...] + grad(lax.rem(z + 3 + i * (Z - 6), Z))))
    b_ag.step(4)
    gt[...] = gt[...] + grad(lax.rem(z + 4, Z))

    mine = pl.ds(pl.multiple_of(c * 8, 8), 8)
    other = pl.ds(pl.multiple_of((1 - c) * 8, 8), 8)
    g_c = rc(gt.at[other], gc, c_s.at[0], c_r.at[0], cdev)
    g_c.start()
    p_ag.step(1)
    g_c.wait_recv()
    gt[mine] += gc[...]
    gr[e] = gt[c * 8 + e]
    e_each(lambda k: e_copy(0, gt.at[c * 8 + k], gr.at[e], k).start())
    p_ag.step(2)

    t_recv(1, q0.at[t], q0r)
    q0a[z] = jnp.sum(q0r[...], axis=0)
    z_send(0, q0a)

    o_add(0)
    o_rs.begin(1)
    e_each(lambda k: rc(gt.at[c * 8 + k], gr.at[k], e_s.at[0, k], e_r.at[0, k], edev(k)).wait_recv())
    gf[c * 8 + e] = jnp.sum(gr[...], axis=0)
    e_each(lambda k: e_copy(1, gf.at[c * 8 + e], gf.at[c * 8 + e], k).start())

    def g_share(k):
        ref = gf.at[c * 8 + k]
        return rc(ref, ref, c_s.at[2 + k], c_r.at[2 + k], cdev)

    g_share(e).start()
    p_ag.step(3)
    o_add(1)
    o_add(2)
    o_rs.begin(2)
    p_ag.step(4)

    gu[...] = jnp.zeros_like(gu)

    @functools.partial(loop, Z)
    def _(k):
        pc = (pag[k].reshape(CH, 128) * delta_multiplier).astype(BF16)
        va = dot_tn(pc, av[tok(k, 0), :])
        vb = dot_tn(pc, av[tok(k, 1), :])
        gu[...] += (va[:64] + vb[64:]).reshape(8, 8, 128)

    gur[e] = gu[e]
    e_each(lambda k: e_copy(2, gu.at[k], gur.at[e], k).start())

    def g_pass(k):
        ref = gf.at[c * 8 + k]
        rc(ref, ref, e_s.at[1, k], e_r.at[1, k], edev(k)).wait_recv()
        g_share(k).start()

    e_each(g_pass)

    def g_share_in(k):
        ref = gf.at[(1 - c) * 8 + k]
        rc(ref, ref, c_s.at[2 + k], c_r.at[2 + k], cdev).wait_recv()

    loop(E, g_share_in)
    ghi, glo = split(gf[...].reshape(128, 1024))
    qk, qv = pack(dot_nt(normed[...], ghi) + dot_nt(normed[...], glo), 128)
    qg[0:8] = qk.reshape(8, 16, 128)
    qg[8:16] = qv.reshape(8, 16, 128)
    qgr[t] = qg[t]
    t_send(2, lambda k: qg.at[k], qgr.at[t])

    o_rs.step(1)
    o_add(3)
    o_add(4)
    e_each(lambda k: rc(gu.at[k], gur.at[k], e_s.at[2, k], e_r.at[2, k], edev(k)).wait_recv())
    guc[c] = jnp.sum(gur[...], axis=0)
    gu_c = rc(guc.at[c], guc.at[c], c_s.at[1], c_r.at[1], cdev)
    gu_c.start()
    o_rs.step(2)
    rc(guc.at[1 - c], guc.at[1 - c], c_s.at[1], c_r.at[1], cdev).wait_recv()
    guf[e] = guc[0] + guc[1]
    e_each(lambda k: e_copy(3, guf.at[e], guf.at[e], k).start())
    o_add(5)
    o_add(6)

    t_recv(2, qg.at[t], qgr)
    qga[z] = jnp.sum(qgr[...], axis=0)
    z_send(1, qga)
    o_rs.step(3)

    e_each(lambda k: rc(guf.at[k], guf.at[k], e_s.at[3, k], e_r.at[3, k], edev(k)).wait_recv())
    g2 = jnp.sum(gf[...] * gf[...], axis=0)
    tile = jnp.sum(guf[...] * guf[...], axis=0)
    for i in range(8):
        tile = tile + g2[:, i * 128 : (i + 1) * 128]
    norms[t] = tile
    t_send(3, lambda k: norms.at[t], norms.at[t])

    o_add(7)
    o_rs.step(4)
    for h in range(2):
        base[h] = o_rs.result(h)
    z_recv(0, q0a)
    z_recv(1, qga)
    t_recv(3, norms.at[t], norms)
    total = jnp.sum(jnp.sum(norms[...], axis=0), keepdims=True)
    factor = jnp.minimum(1.0, clip_limit / (jnp.sqrt(total) + 1e-06))
    q = q0a[...].reshape(128, 128) - learning_rate * factor * qga[...].reshape(128, 128)
    up = uv[...] - learning_rate * factor * guf[...].reshape(64, 128)
    zero = jnp.zeros_like(up)
    for h in range(2):
        wide = jnp.concatenate([up, zero] if h == 0 else [zero, up], axis=0)
        v = jnp.dot(q, wide, precision=lax.Precision.HIGHEST, preferred_element_type=F32)
        o_ref[:, h * 128 : (h + 1) * 128] = jnp.transpose(base[h] + delta_multiplier * v)

    b_rs.drain()
    b_ag.drain()
    p_rs.drain()
    p_ag.drain()
    o_rs.drain()
    b_y.wait_send()

    @functools.partial(loop, Z)
    def _(j):
        p_y(j).wait_send()
        o_y(j).wait_send()
        g_share(j).wait_send()

    t_drain(0, lambda k: rows.at[t], rows.at[t])
    t_drain(1, lambda k: q0.at[k], q0r.at[t])
    t_drain(2, lambda k: qg.at[k], qgr.at[t])
    t_drain(3, lambda k: norms.at[t], norms.at[t])

    @functools.partial(loop, Z - 1)
    def _(i):
        z_copy(0, q0a, i).wait_send()
        z_copy(1, qga, i).wait_send()

    def e_drain(k):
        e_copy(0, gt.at[c * 8 + k], gr.at[e], k).wait_send()
        e_copy(1, gf.at[c * 8 + e], gf.at[c * 8 + e], k).wait_send()
        e_copy(2, gu.at[k], gur.at[e], k).wait_send()
        e_copy(3, guf.at[e], guf.at[e], k).wait_send()

    e_each(e_drain)
    g_c.wait_send()
    gu_c.wait_send()


def shards(x, a, w, d, u, hidden, gain):
    V = pltpu.VMEM
    dma = pltpu.SemaphoreType.DMA
    part = (8, 2, 96, 128)
    scratch = [
        V((3072, 1024), BF16), V((3072, 128), BF16), V((1024, 2048), BF16), V((1024, 128), F32),
        V((64, 128), F32), V((256, 1024), BF16), V((1, 1024), F32), V((1024, 128), BF16), V((64, 128), BF16),
        V(part, F32), V((2, 4, 2, 96, 128), F32), V((8, 2, 192, 128), F32),
        V(part, F32), V(part, F32), V(part, F32), V((2, 4, 2, 96, 128), F32), V(part, F32),
        V((16, 2, 128, 128), F32), V((8, 2, 128, 128), F32), V((2, 4, 2, 128, 128), F32),
        V((16, 8, 1024), F32), V((8, 8, 1024), F32), V((8, 8, 1024), F32), V((16, 8, 1024), F32),
        V((8, 8, 128), F32), V((8, 8, 128), F32), V((2, 8, 128), F32), V((8, 8, 128), F32),
        V((16, 8, 256), F32), V((16, 8, 128), F32), V((256, 1024), BF16), V((2, 128, 128), F32),
        V((16, 16, 128), F32), V((16, 16, 128), F32), V((8, 16, 128), F32),
        V((16, 16, 128), F32), V((16, 16, 128), F32), V((8, 16, 128), F32),
        dma((6,)), dma((8, 2)), dma((5, 2, 2, 4)), dma((5, 2, 2, 4)), dma((3, 8)), dma((3, 8)),
        dma((4, 16)), dma((4, 16)), dma((2, 8)), dma((2, 8)), dma((4, 8)), dma((4, 8)), dma((10,)), dma((10,)),
    ]
    return pl.pallas_call(
        kernel,
        out_shape=jax.ShapeDtypeStruct((128, 256), F32),
        in_specs=[pl.BlockSpec(memory_space=pl.ANY)] * 7,
        out_specs=pl.BlockSpec(memory_space=pltpu.VMEM),
        scratch_shapes=scratch,
        compiler_params=pltpu.CompilerParams(
            collective_id=0, has_side_effects=True, vmem_limit_bytes=56 << 20
        ),
    )(x, a, w, d, u, hidden, gain.reshape(1, 1024))


def solution(mesh):
    placed = (
        P("dp", "tensor"),
        P("dp", "tensor"),
        P("tensor", None),
        P("tensor", None),
        P(None, "tensor"),
        P("dp", "tensor"),
        P("tensor"),
    )
    return jax.shard_map(
        shards, mesh=mesh, in_specs=placed, out_specs=P("tensor", "dp"), check_vma=False
    )
```

time: 472 us -> 100 us (0.21)
  the two profiles are of different devices: /device:TPU:6 before, /device:TPU:1 now
where the time goes in v1:
time: 100 us
  Pallas kernels  98.6 us (99%)
  local copies, waits for them, and re-layouts  1.57 us (2%)
    pallas_call x1, Pallas kernels, shards(): pl.pallas_call(kernel, out_shape=jax.ShapeDtypeStruct((128, 256), F32), i...  98.6 us

profile of v1, /device:TPU:1, one launch (start us, length us, event | category | flops | bytes accessed | tf_op | source)
XLA Modules:
  0.0 100.2 jit_solution(10830110099793261661)
XLA Ops:
  0.0 98.6 %shard_map.73 = f32[128,256]{1,0:T(8,128)} custom-call(bf16[3072,1024]{1,0:T(8,128)(2,1)} %x_hbm.1, bf16[3072,128]{1,0:T(8,128)(2,1)} %a_hbm.1, bf16[1024,2048]{1,0:T(8,128)(2,1)} %w_hbm.1, f32[1024,128]{1,0:T(8,128)} %d_hbm.1, f32[64,128]{1,0:T(8,128)} %u_hbm.1, bf16[256,1024]{1,0:T(8,128)(2,1)} %h_hbm.1, f32[1,1024]{1,0:T(1,128)} %bitcast.1), custom_call_target="tpu_custom_call" | custom-call | tf_op jit(solution)/shard_map/pallas_call | solution.py:543
  98.6 1.6 %copy.9 = f32[128,256]{1,0:T(8,128)} copy(f32[128,256]{1,0:T(8,128)} %shard_map.73) | data formatting | bytes 262144

commit v2 on v1

v2 whole, which is shorter than its diff:
```python
import functools

import jax
import jax.numpy as jnp
from jax import lax
from jax.experimental import pallas as pl
from jax.experimental.pallas import tpu as pltpu
from jax.sharding import PartitionSpec as P

MESH = pl.DeviceIdType.MESH
F32 = jnp.float32
BF16 = jnp.bfloat16

EMBED_DIMENSION = 16384
delta_multiplier = 2.0
learning_rate = 4.0
clip_limit = 1.0

Z = 8
T = 16
E = 8
CH = 192


def rc(src, dst, ss, rs, dev):
    return pltpu.make_async_remote_copy(
        src_ref=src, dst_ref=dst, send_sem=ss, recv_sem=rs, device_id=dev, device_id_type=MESH
    )


def low_lanes(rows):
    return lax.broadcasted_iota(jnp.int32, (rows, 128), 1) < 64


def swap(v):
    return pltpu.roll(v, 64, 1)


def dot(a, b):
    return jnp.dot(a, b, preferred_element_type=F32)


def dot_nt(a, b):
    return lax.dot_general(a, b, (((1,), (1,)), ((), ())), preferred_element_type=F32)


def dot_tn(a, b):
    return lax.dot_general(a, b, (((0,), (0,)), ((), ())), preferred_element_type=F32)


def split(v):
    hi = v.astype(BF16)
    return hi, (v - hi.astype(F32)).astype(BF16)


class RingReduce:
    def __init__(self, own, buf, ss, rs, z, dev):
        self.own, self.buf, self.ss, self.rs, self.z, self.dev = own, buf, ss, rs, z, dev

    def chunk(self, d, far):
        return lax.rem(self.z + (far if d == 0 else Z - far), Z)

    def slot(self, d, h, s):
        return d * 7 + (s - 1 if d == h else 4 + s - 2)

    def copy(self, d, h, s):
        first = 1 if d == h else 2
        if s == first:
            src = self.own(self.chunk(d, 5 - s), h)
        else:
            src = self.buf.at[self.slot(d, h, s - 1)]
        i = self.slot(d, h, s)
        return rc(src, self.buf.at[i], self.ss, self.rs.at[i], self.dev(d))

    def begin(self, first):
        for d in range(2):
            h = d if first == 1 else 1 - d
            self.copy(d, h, first).start()

    def step(self, s):
        for same in (True, False):
            if s == 1 and not same:
                continue
            for d in range(2):
                h = d if same else 1 - d
                self.copy(d, h, s).wait_recv()
                if s < 4:
                    self.buf[self.slot(d, h, s)] += self.own(self.chunk(d, 4 - s), h)[...]
                    self.copy(d, h, s + 1).start()

    def result(self, h):
        return self.own(self.z, h)[...] + (self.buf[self.slot(0, h, 4)] + self.buf[self.slot(1, h, 4)])

    def drain(self):
        rc(self.buf, self.buf, self.ss, self.rs.at[0], self.dev(0)).wait_send()


class RingGather:
    def __init__(self, arr, ss, rs, z, dev):
        self.arr, self.ss, self.rs, self.z, self.dev = arr, ss, rs, z, dev

    def copy(self, d, p, s):
        k = lax.rem(self.z + (Z - (s - 1) if d == 0 else s - 1), Z)
        ref = self.arr.at[k, p]
        i = d * 7 + (s - 1 if d == p else 4 + s - 1)
        return rc(ref, ref, self.ss, self.rs.at[i], self.dev(d))

    def begin(self, p):
        for d in range(2):
            self.copy(d, p, 1).start()

    def step(self, p, s):
        for d in (p, 1 - p):
            last = 4 if d == p else 3
            if s <= last:
                self.copy(d, p, s).wait_recv()
                if s + 1 <= last:
                    self.copy(d, p, s + 1).start()

    def drain(self):
        all_sent = self.arr.at[0:7]
        rc(all_sent, all_sent, self.ss, self.rs.at[0], self.dev(0)).wait_send()


def kernel(
    x_hbm, a_hbm, w_hbm, d_hbm, u_hbm, h_hbm, gain_hbm, o_ref,
    xv, av, wv, dv, uv, hv, gv, db, ub,
    bm, br, bag, pm, pt, py, pr, pag, om, oy, orr,
    gt, gc, gr, gf, gu, guc, gur, guf, rows, norms, normed, base,
    q0a, qg, qgr, qga,
    ld, xs, ring_r, py_r, oy_r, y_r, t_r, z_r, e_r, c_r, sent,
):
    dpi = lax.axis_index("dp")
    t = lax.axis_index("tensor")
    e, c = dpi // 2, lax.rem(dpi, 2)
    y, z = t // Z, lax.rem(t, Z)
    zdev = (dpi, y * Z + lax.rem(z + 1, Z)), (dpi, y * Z + lax.rem(z + Z - 1, Z))
    ydev = (dpi, (1 - y) * Z + z)
    cdev = (e * 2 + 1 - c, t)

    def ring(d):
        return zdev[d]

    def tdev(k):
        return (dpi, k)

    def edev(k):
        return (k * 2 + c, t)

    def order(j):
        far = 4 - (j + 1) // 2
        return lax.rem(z + (1 - 2 * lax.rem(j + 1, 2)) * far + Z, Z)

    def loop(n, body, first=0):
        def step(i, carry):
            body(i)
            return carry

        lax.fori_loop(first, n, step, 0)

    def both(far, body):
        if far in (0, 4):
            body(lax.rem(z + far, Z))
        else:
            loop(2, lambda i: body(lax.rem(z + far + i * (Z - 2 * far), Z)))

    def local(src, dst, i):
        return pltpu.make_async_copy(src, dst, ld.at[i])

    l_u, l_a, l_d = local(u_hbm, uv, 0), local(a_hbm, av, 1), local(d_hbm, dv, 2)
    l_h, l_g, l_w = local(h_hbm, hv, 3), local(gain_hbm, gv, 4), local(w_hbm, wv, 5)

    def xload(j):
        k = order(j)
        return pltpu.make_async_copy(x_hbm.at[:, k], xv.at[:, k], xs.at[j])

    l_u.start()
    l_a.start()
    l_d.start()
    loop(Z, lambda j: xload(j).start())
    l_h.start()
    l_g.start()
    l_w.start()

    barrier = pltpu.get_barrier_semaphore()

    def hello(dev):
        pl.semaphore_signal(barrier, inc=1, device_id=dev, device_id_type=MESH)

    hello(cdev)
    loop(T - 1, lambda i: hello(tdev(lax.rem(t + 1 + i, T))))
    loop(E - 1, lambda i: hello(edev(lax.rem(e + 1 + i, E))))

    b_rs = RingReduce(lambda k, h: bm.at[k, h], br, sent.at[0], ring_r.at[0], z, ring)
    b_ag = RingGather(bag, sent.at[1], ring_r.at[1], z, ring)
    p_rs = RingReduce(lambda k, h: pm.at[k, h], pr, sent.at[2], ring_r.at[2], z, ring)
    p_ag = RingGather(pag, sent.at[3], ring_r.at[3], z, ring)
    o_rs = RingReduce(lambda k, h: om.at[y * Z + k, h], orr, sent.at[4], ring_r.at[4], z, ring)

    def p_y(j):
        k = order(j)
        return rc(pt.at[k], py.at[k], sent.at[5], py_r.at[j], ydev)

    def o_y(j):
        k = order(j)
        return rc(om.at[(1 - y) * Z + k], oy.at[k], sent.at[6], oy_r.at[j], ydev)

    b_y = rc(bag.at[z, 0], bag.at[z, 1], sent.at[7], y_r.at[0], ydev)

    def p_add(j):
        p_y(j).wait_recv()
        k = order(j)
        pm[k] += py[k]

    def o_add(j):
        o_y(j).wait_recv()
        k = order(j)
        om[y * Z + k] += oy[k]

    def t_copy(n, ref, k):
        return rc(ref, ref, sent.at[9 + n], t_r.at[n], tdev(k))

    def t_send(n, ref):
        loop(T - 1, lambda i: t_copy(n, ref, lax.rem(t + 1 + i, T)).start())

    def t_all(n, some):
        return t_copy(n, some, lax.rem(t + 1, T))

    def z_copy(n, src, dst, k, side=0):
        return rc(src, dst, sent.at[11 + n], z_r.at[n], tdev((y + side - 2 * y * side) * Z + k))

    def z_others(body):
        loop(Z - 1, lambda i: body(lax.rem(z + 1 + i, Z)))

    def z_gather(n, arr):
        z_others(lambda k: z_copy(n, arr.at[z], arr.at[z], k).start())

    def z_all(n, some, side=0):
        return z_copy(n, some, some, lax.rem(z + 1, Z), side)

    def e_copy(n, src, dst, k):
        return rc(src, dst, sent.at[16 + n], e_r.at[n], edev(k))

    def e_others(body):
        loop(E - 1, lambda i: body(lax.rem(e + 1 + i, E)))

    def e_all(n, some):
        return e_copy(n, some, some, lax.rem(e + 1, E))

    def c_copy(n, src, dst):
        return rc(src, dst, sent.at[21 + n], c_r.at[n], cdev)

    l_u.wait()
    l_a.wait()
    ub[...] = uv[...].astype(BF16)
    blank = jnp.zeros((64, 128), BF16)

    def back(j):
        k = order(j)
        u1 = jnp.concatenate([ub[...], blank], axis=0)
        u2 = jnp.concatenate([blank, ub[...]], axis=0)
        v = dot_nt(av[0, k], u1) + dot_nt(av[1, k], u2)
        bm[k] = v.reshape(2, CH // 2, 128)

    loop(3, back)
    pl.semaphore_wait(barrier, T - 1 + E - 1 + 1)
    b_rs.begin(1)
    b_rs.begin(2)
    loop(Z, back, 3)

    l_d.wait()
    dd = dv[...]
    db[...] = jnp.where(y == 0, dd, swap(dd)).astype(BF16)

    def project(j):
        k = order(j)
        xload(j).wait()
        pa = dot(xv[0, k], db[...])
        pb = dot(xv[1, k], db[...])
        low = low_lanes(CH)
        pm[k] = jnp.where(low, pa, swap(pb)).reshape(2, CH // 2, 128)
        pt[k] = jnp.where(low, swap(pa), pb).reshape(2, CH // 2, 128)

    def project_send(j):
        project(j)
        p_y(j).start()

    loop(4, project_send)
    b_rs.step(1)
    loop(6, project_send, 4)
    loop(8, project, 6)
    p_add(0)
    p_rs.begin(1)

    l_h.wait()
    l_g.wait()
    hf = hv[...].astype(F32)
    sq = jnp.sum(hf * hf, axis=1, keepdims=True)
    sq = jnp.transpose(jnp.broadcast_to(sq, (256, 128)))
    rows[t, 0:1] = sq[0:1, 0:128]
    rows[t, 1:2] = sq[0:1, 128:256]
    t_send(0, rows.at[t])

    b_rs.step(2)
    p_add(1)
    b_rs.step(3)
    p_add(2)
    p_rs.begin(2)
    p_rs.step(1)
    b_rs.step(4)
    for h in range(2):
        bag[z, 0, h * 96 : (h + 1) * 96] = b_rs.result(h)
    b_ag.begin(0)
    b_y.start()
    loop(8, lambda j: p_y(j).start(), 6)

    def grad(p, k):
        cot = (bag[k, p] * delta_multiplier).astype(BF16)
        v = dot_tn(cot[:, :64], xv[0, k]) + dot_tn(cot[:, 64:], xv[1, k])
        gt[p, 0] += v[:, :512].reshape(8, 8, 512)
        gt[p, 1] += v[:, 512:].reshape(8, 8, 512)

    gt[...] = jnp.zeros_like(gt)
    both(0, lambda k: grad(0, k))

    t_all(0, rows.at[0:15]).wait_recv()
    mean = jnp.sum(rows[...], axis=0) / EMBED_DIMENSION
    scale = lax.rsqrt(mean + 1e-05)
    for i in range(2):
        half = slice(i * 128, (i + 1) * 128)
        col = jnp.transpose(jnp.broadcast_to(scale[i : i + 1], (128, 128)))
        for n in range(8):
            sl = slice(n * 128, (n + 1) * 128)
            normed[half, sl] = (hv[half, sl].astype(F32) * col * gv[:, sl]).astype(BF16)

    p_add(3)
    p_add(4)
    p_rs.step(2)
    b_ag.step(0, 1)
    b_y.wait_recv()
    b_ag.begin(1)

    def pack(v):
        return jnp.where(low_lanes(128), v[:128], v[128:]).reshape(8, 2, 8, 128)

    def twice(v, p):
        keep = low_lanes(256) if p == 0 else jnp.logical_not(low_lanes(256))
        v = jnp.where(keep, v, 0.0)
        return v + swap(v)

    def out_pair(i):
        v = dot(normed[...], wv[:, pl.ds(pl.multiple_of(i * 256, 256), 256)])
        om[2 * i, :, 0:128] = v[:, :128].reshape(2, 128, 128)
        om[2 * i + 1, :, 0:128] = v[:, 128:].reshape(2, 128, 128)

    dhi, dlo = split(dv[...])
    v = dot(normed[...], dhi) + dot(normed[...], dlo)
    for side in range(2):
        om[side * Z : side * Z + Z, :, 128:136] = pack(twice(v, side))
    l_w.wait()
    loop(4, lambda i: out_pair((1 - y) * 4 + i))
    loop(2, lambda j: o_y(j).start())
    both(1, lambda k: grad(0, k))
    b_ag.step(0, 2)
    p_add(5)
    p_add(6)
    p_rs.step(3)
    both(0, lambda k: grad(1, k))
    both(2, lambda k: grad(0, k))
    b_ag.step(1, 1)
    loop(3, lambda j: o_y(j).start(), 2)
    loop(4, lambda i: out_pair(y * 4 + i))
    b_ag.step(0, 3)
    p_add(7)
    p_rs.step(4)
    for h in range(2):
        pag[z, h] = p_rs.result(h)
    both(3, lambda k: grad(0, k))
    b_ag.step(1, 2)
    loop(4, lambda j: o_y(j).start(), 3)
    b_ag.step(0, 4)
    p_ag.begin(0)
    p_ag.begin(1)
    both(4, lambda k: grad(0, k))

    def g_core(p):
        return c_copy(p, gt.at[p, 1 - c], gc.at[p])

    def g_reduce(p):
        g_core(p).wait_recv()
        gt[p, c] += gc[p]
        gr[p, e] = gt[p, c, e]
        e_others(lambda k: e_copy(p, gt.at[p, c, k], gr.at[p, e], k).start())

    def g_gather(p):
        e_all(p, gr.at[p, 0:7]).wait_recv()
        gf[p, c, e] = jnp.sum(gr[p], axis=0)
        ref = gf.at[p, c, e]
        e_others(lambda k: e_copy(2 + p, ref, ref, k).start())

    def g_share(p):
        return c_copy(2 + p, gf.at[p, c], gf.at[p, c])

    def g_pass(p):
        e_all(2 + p, gf.at[p, c, 0:7]).wait_recv()
        g_share(p).start()

    def up_grad(k):
        pc = (pag[k].reshape(CH, 128) * delta_multiplier).astype(BF16)
        va = dot_tn(pc, av[0, k])
        vb = dot_tn(pc, av[1, k])
        gu[...] += (va[:64] + vb[64:]).reshape(8, 8, 128)

    def q_of(p):
        ghi, glo = split(jnp.concatenate([gf[p, 0].reshape(64, 512), gf[p, 1].reshape(64, 512)], axis=1))
        v = dot_nt(normed[...], jnp.concatenate([ghi, glo], axis=0))
        qg[p] = pack(v + swap(v)).reshape(8, 16, 128)

    theirs = [gf.at[p, 1 - c] for p in range(2)]

    g_core(0).start()
    both(1, lambda k: grad(1, k))
    gu[...] = jnp.zeros_like(gu)
    b_ag.step(1, 3)
    loop(6, lambda j: o_y(j).start(), 4)
    o_add(0)
    o_rs.begin(1)
    g_reduce(0)
    both(2, lambda k: grad(1, k))
    both(3, lambda k: grad(1, k))
    both(0, up_grad)
    b_ag.step(1, 4)
    both(4, lambda k: grad(1, k))
    g_core(1).start()
    p_ag.step(0, 1)
    p_ag.step(1, 1)
    o_add(1)
    o_add(2)
    o_rs.begin(2)
    both(1, up_grad)
    g_reduce(1)
    g_gather(0)
    o_rs.step(1)
    p_ag.step(0, 2)
    p_ag.step(1, 2)
    loop(7, lambda j: o_y(j).start(), 6)
    both(2, up_grad)
    o_add(3)
    o_add(4)
    o_rs.step(2)
    g_pass(0)
    g_gather(1)
    p_ag.step(0, 3)
    p_ag.step(1, 3)
    loop(8, lambda j: o_y(j).start(), 7)
    both(3, up_grad)
    c_copy(2, theirs[0], theirs[0]).wait_recv()
    q_of(0)
    qgr[0, z] = qg[0, z]
    z_others(lambda k: z_copy(3, qg.at[0, k], qgr.at[0, z], k).start())
    p_ag.step(0, 4)
    p_ag.step(1, 4)
    both(4, up_grad)
    gu_c = c_copy(4, gu, guc)
    gu_c.start()
    g_pass(1)
    o_add(5)
    o_add(6)
    gu_c.wait_recv()
    gur[e] = gu[...] + guc[...]
    e_others(lambda k: e_copy(4, gur.at[e], gur.at[e], k).start())
    c_copy(3, theirs[1], theirs[1]).wait_recv()
    q_of(1)
    loop(Z, lambda i: z_copy(4, qg.at[1, lax.rem(z + i, Z)], qgr.at[1, z], lax.rem(z + i, Z), 1).start())
    o_rs.step(3)
    g2 = jnp.sum(gf[...] * gf[...], axis=(0, 1, 2))
    tile = g2[:, 0:128] + g2[:, 128:256] + g2[:, 256:384] + g2[:, 384:512]
    o_add(7)
    e_all(4, gur.at[0:7]).wait_recv()
    guf[...] = jnp.sum(gur[...], axis=0)
    norms[t] = jnp.sum(tile + jnp.sum(guf[...] * guf[...], axis=0), axis=0, keepdims=True)
    t_send(1, norms.at[t])
    z_all(3, qgr.at[0, 0:7]).wait_recv()
    z_all(4, qgr.at[1], 1).wait_recv()
    qga[z] = jnp.sum(qgr[0], axis=0) + jnp.sum(qgr[1], axis=0)
    z_gather(2, qga)
    o_rs.step(4)
    for h in range(2):
        v = o_rs.result(h)
        base[h] = v[0:128]
        q0a[z, h * 8 : h * 8 + 8] = v[128:136]
    z_gather(1, q0a)
    t_all(1, norms.at[0:15]).wait_recv()
    total = jnp.sum(jnp.sum(norms[...], axis=0), keepdims=True)
    factor = jnp.minimum(1.0, clip_limit / (jnp.sqrt(total) + 1e-06))
    up = uv[...] - learning_rate * factor * guf[...].reshape(64, 128)
    zero = jnp.zeros_like(up)
    z_all(2, qga.at[0:7]).wait_recv()
    z_all(1, q0a.at[0:7]).wait_recv()
    q = q0a[...].reshape(128, 128) - learning_rate * factor * qga[...].reshape(128, 128)
    for h in range(2):
        wide = jnp.concatenate([up, zero] if h == 0 else [zero, up], axis=0)
        v = jnp.dot(q, wide, precision=lax.Precision.HIGHEST, preferred_element_type=F32)
        o_ref[:, h * 128 : (h + 1) * 128] = jnp.transpose(base[h] + delta_multiplier * v)

    for exchange in (b_rs, b_ag, p_rs, p_ag, o_rs):
        exchange.drain()
    rc(py, py, sent.at[5], py_r.at[0], ydev).wait_send()
    rc(oy, oy, sent.at[6], oy_r.at[0], ydev).wait_send()
    b_y.wait_send()
    t_all(0, rows.at[0:15]).wait_send()
    t_all(1, norms.at[0:15]).wait_send()
    z_all(1, q0a.at[0:7]).wait_send()
    z_all(2, qga.at[0:7]).wait_send()
    z_all(3, qgr.at[0, 0:7]).wait_send()
    z_all(4, qgr.at[1], 1).wait_send()
    for p in range(2):
        e_all(p, gr.at[p, 0:7]).wait_send()
        e_all(2 + p, gf.at[p, c, 0:7]).wait_send()
        g_core(p).wait_send()
        g_share(p).wait_send()
    e_all(4, gur.at[0:7]).wait_send()
    gu_c.wait_send()


def shards(x, a, w, d, u, hidden, gain):
    V = pltpu.VMEM
    dma = pltpu.SemaphoreType.DMA
    part = (8, 2, 96, 128)
    scratch = [
        V((2, 8, 192, 1024), BF16), V((2, 8, 192, 128), BF16), V((1024, 2048), BF16), V((1024, 128), F32),
        V((64, 128), F32), V((256, 1024), BF16), V((1, 1024), F32), V((1024, 128), BF16), V((64, 128), BF16),
        V(part, F32), V((14, 96, 128), F32), V((8, 2, 192, 128), F32),
        V(part, F32), V(part, F32), V(part, F32), V((14, 96, 128), F32), V(part, F32),
        V((16, 2, 136, 128), F32), V((8, 2, 136, 128), F32), V((14, 136, 128), F32),
        V((2, 2, 8, 8, 512), F32), V((2, 8, 8, 512), F32), V((2, 8, 8, 512), F32), V((2, 2, 8, 8, 512), F32),
        V((8, 8, 128), F32), V((8, 8, 128), F32), V((8, 8, 8, 128), F32), V((8, 8, 128), F32),
        V((16, 2, 128), F32), V((16, 1, 128), F32), V((256, 1024), BF16), V((2, 128, 128), F32),
        V((8, 16, 128), F32),
        V((2, 8, 16, 128), F32), V((2, 8, 16, 128), F32), V((8, 16, 128), F32),
        dma((6,)), dma((8,)), dma((5, 14)), dma((8,)), dma((8,)), dma((2,)),
        dma((2,)), dma((5,)), dma((5,)), dma((5,)), dma((26,)),
    ]
    return pl.pallas_call(
        kernel,
        out_shape=jax.ShapeDtypeStruct((128, 256), F32),
        in_specs=[pl.BlockSpec(memory_space=pl.ANY)] * 7,
        out_specs=pl.BlockSpec(memory_space=pltpu.VMEM),
        scratch_shapes=scratch,
        compiler_params=pltpu.CompilerParams(
            collective_id=0, has_side_effects=True, vmem_limit_bytes=56 << 20
        ),
    )(x.reshape(2, 8, CH, 1024), a.reshape(2, 8, CH, 128), w, d, u, hidden, gain.reshape(1, 1024))


def solution(mesh):
    placed = (
        P("dp", "tensor"),
        P("dp", "tensor"),
        P("tensor", None),
        P("tensor", None),
        P(None, "tensor"),
        P("dp", "tensor"),
        P("tensor"),
    )
    return jax.shard_map(
        shards, mesh=mesh, in_specs=placed, out_specs=P("tensor", "dp"), check_vma=False
    )
```

time: 100 us -> 84.9 us (0.85)
  Pallas kernels: 98.6 us -> 83.3 us
    pallas_call x1, Pallas kernels: 98.6 us -> 83.3 us  [shards(): pl.pallas_call(kernel, out_shape=jax.ShapeDtypeStruct((128, 256), F32), i...]
where the time goes in v2:
time: 84.9 us; the launch traced here: 84.8 us
  Pallas kernels  83.3 us (98%)
  local copies, waits for them, and re-layouts  1.57 us (2%)
    pallas_call x1, Pallas kernels, shards(): pl.pallas_call(kernel, out_shape=jax.ShapeDtypeStruct((128, 256), F32), i...  83.3 us

profile of v2, /device:TPU:1, one launch (start us, length us, event | category | flops | bytes accessed | tf_op | source)
XLA Modules:
  0.0 84.8 jit_solution(8287352219270070839)
XLA Ops:
  0.0 83.3 %shard_map.73 = f32[128,256]{1,0:T(8,128)} custom-call(bf16[2,8,192,1024]{3,2,1,0:T(8,128)(2,1)} %bitcast.3, bf16[2,8,192,128]{3,2,1,0:T(8,128)(2,1)} %bitcast.4, bf16[1024,2048]{1,0:T(8,128)(2,1)} %w_hbm.1, f32[1024,128]{1,0:T(8,128)} %d_hbm.1, f32[64,128]{1,0:T(8,128)} %u_hbm.1, bf16[256,1024]{1,0:T(8,128)(2,1)} %h_hbm.1, f32[1,1024]{1,0:T(1,128)} %bitcast.5), custom_call_target="tpu_custom_call" | custom-call | tf_op jit(solution)/shard_map/pallas_call | solution.py:544
  83.3 1.6 %copy.9 = f32[128,256]{1,0:T(8,128)} copy(f32[128,256]{1,0:T(8,128)} %shard_map.73) | data formatting | bytes 262144

commit v3 on v2

v3 whole, which is shorter than its diff:
```python
import functools

import jax
import jax.numpy as jnp
from jax import lax
from jax.experimental import pallas as pl
from jax.experimental.pallas import tpu as pltpu
from jax.sharding import PartitionSpec as P

MESH = pl.DeviceIdType.MESH
F32 = jnp.float32
BF16 = jnp.bfloat16

EMBED_DIMENSION = 16384
delta_multiplier = 2.0
learning_rate = 4.0
clip_limit = 1.0

Z = 8
T = 16
E = 8
CH = 192


def rc(src, dst, ss, rs, dev):
    return pltpu.make_async_remote_copy(
        src_ref=src, dst_ref=dst, send_sem=ss, recv_sem=rs, device_id=dev, device_id_type=MESH
    )


def low_lanes(rows):
    return lax.broadcasted_iota(jnp.int32, (rows, 128), 1) < 64


def swap(v):
    return pltpu.roll(v, 64, 1)


def dot(a, b):
    return jnp.dot(a, b, preferred_element_type=F32)


def dot_nt(a, b):
    return lax.dot_general(a, b, (((1,), (1,)), ((), ())), preferred_element_type=F32)


def dot_tn(a, b):
    return lax.dot_general(a, b, (((0,), (0,)), ((), ())), preferred_element_type=F32)


def split(v):
    hi = v.astype(BF16)
    return hi, (v - hi.astype(F32)).astype(BF16)


class RingReduce:
    def __init__(self, own, buf, ss, rs, z, dev):
        self.own, self.buf, self.ss, self.rs, self.z, self.dev = own, buf, ss, rs, z, dev

    def chunk(self, d, far):
        return lax.rem(self.z + (far if d == 0 else Z - far), Z)

    def slot(self, d, h, s):
        return d * 7 + (s - 1 if d == h else 4 + s - 2)

    def copy(self, d, h, s):
        first = 1 if d == h else 2
        if s == first:
            src = self.own(self.chunk(d, 5 - s), h)
        else:
            src = self.buf.at[self.slot(d, h, s - 1)]
        i = self.slot(d, h, s)
        return rc(src, self.buf.at[i], self.ss, self.rs.at[i], self.dev(d))

    def begin(self, first):
        for d in range(2):
            h = d if first == 1 else 1 - d
            self.copy(d, h, first).start()

    def step(self, s):
        for same in (True, False):
            if s == 1 and not same:
                continue
            for d in range(2):
                h = d if same else 1 - d
                self.copy(d, h, s).wait_recv()
                if s < 4:
                    self.buf[self.slot(d, h, s)] += self.own(self.chunk(d, 4 - s), h)[...]
                    self.copy(d, h, s + 1).start()

    def result(self, h):
        return self.own(self.z, h)[...] + (self.buf[self.slot(0, h, 4)] + self.buf[self.slot(1, h, 4)])

    def drain(self):
        rc(self.buf, self.buf, self.ss, self.rs.at[0], self.dev(0)).wait_send()


class RingGather:
    def __init__(self, arr, ss, rs, z, dev, dev2):
        self.arr, self.ss, self.rs, self.z, self.dev, self.dev2 = arr, ss, rs, z, dev, dev2

    def copy(self, d, p, s):
        k = lax.rem(self.z + (0, Z - 1, Z - 2, Z - 2)[s - 1] if d == 0 else self.z + (0, 1, 2, 2)[s - 1], Z)
        ref = self.arr.at[k, p]
        i = d * 7 + (s - 1 if d == p else 4 + s - 1)
        return rc(ref, ref, self.ss, self.rs.at[i], (self.dev2 if s == 4 else self.dev)(d))

    def begin(self):
        for p in range(2):
            for d in range(2):
                self.copy(d, p, 1).start()

    def step(self, s):
        for same in (True, False):
            for d in range(2):
                p = d if same else 1 - d
                self.copy(d, p, s).wait_recv()
                if s == 2 and same:
                    self.copy(d, p, 4).start()
                if s < 3:
                    self.copy(d, p, s + 1).start()
        if s == 3:
            for d in range(2):
                self.copy(d, d, 4).wait_recv()

    def drain(self):
        all_sent = self.arr.at[0:7]
        rc(all_sent, all_sent, self.ss, self.rs.at[0], self.dev(0)).wait_send()


class ShortRingReduce:
    def __init__(self, own, buf, ss, rs, z, dev, dev2):
        self.own, self.buf, self.ss, self.rs, self.z, self.dev, self.dev2 = own, buf, ss, rs, z, dev, dev2

    def chunk(self, d, far):
        return lax.rem(self.z + (far if d == 0 else Z - far), Z)

    def copy(self, d, h, s):
        i = d * 7 + 2 * s - 1 + h
        src = self.own(self.chunk(d, 3), h) if s == 1 else self.buf.at[i - 2]
        return rc(src, self.buf.at[i], self.ss, self.rs.at[i], self.dev(d))

    def antipode(self, d):
        i = d * 7
        return rc(self.own(self.chunk(d, 4), d), self.buf.at[i], self.ss, self.rs.at[i], self.dev2(d))

    def begin(self, same):
        for d in range(2):
            self.copy(d, d if same else 1 - d, 1).start()

    def step(self, s):
        for same in (True, False):
            for d in range(2):
                h = d if same else 1 - d
                self.copy(d, h, s).wait_recv()
                if s == 3:
                    continue
                v = self.own(self.chunk(d, 3 - s), h)[...]
                if s == 1 and same:
                    self.antipode(d).wait_recv()
                    v = v + self.buf[d * 7]
                self.buf[d * 7 + 2 * s - 1 + h] += v
                self.copy(d, h, s + 1).start()

    def result(self, h):
        return self.own(self.z, h)[...] + (self.buf[5 + h] + self.buf[12 + h])

    def drain(self):
        rc(self.buf, self.buf, self.ss, self.rs.at[0], self.dev(0)).wait_send()


class PairRingGather:
    def __init__(self, arr, ss, ss4, rs, z, dev):
        self.arr, self.ss, self.ss4, self.rs, self.z, self.dev = arr, ss, ss4, rs, z, dev

    def copy(self, d, p, s):
        k = lax.rem(self.z + (Z - s + 1 if d == 0 else s - 1), Z)
        ref = self.arr.at[k, p, d * 96 : d * 96 + 96] if s == 4 else self.arr.at[k, p]
        return rc(ref, ref, self.ss4 if s == 4 else self.ss, self.rs.at[d * 6 + p * 4 + s - 1], self.dev(d))

    def begin(self, p):
        for d in range(2):
            self.copy(d, p, 1).start()

    def step(self, p, s):
        for d in range(2):
            self.copy(d, p, s).wait_recv()
            if s < (4, 2)[p]:
                self.copy(d, p, s + 1).start()

    def drain(self):
        for ref, ss in ((self.arr.at[0:5], self.ss), (self.arr.at[0, 0], self.ss4)):
            rc(ref, ref, ss, self.rs.at[0], self.dev(0)).wait_send()


def kernel(
    x_hbm, a_hbm, w_hbm, d_hbm, u_hbm, h_hbm, gain_hbm, o_ref,
    xv, av, wv, dv, uv, hv, gv, db, ub,
    bm, br, bag, pm, pt, py, pr, pag, om, oy, orr,
    gt, gr, gh, gf, gu, gur, guh, guf, rows, norms, normed, base,
    q0, q0y, q0r, q0a, qg, qgr, qga,
    ld, ls, xs, ring_r, py_r, oy_r, y_r, t_r, z_r, w_r, h_r, sent,
):
    dpi = lax.axis_index("dp")
    t = lax.axis_index("tensor")
    e, c = dpi // 2, lax.rem(dpi, 2)
    xx, yh = e // 2, lax.rem(e, 2)
    y, z = t // Z, lax.rem(t, Z)
    zdev = (dpi, y * Z + lax.rem(z + 1, Z)), (dpi, y * Z + lax.rem(z + Z - 1, Z))
    ydev = (dpi, (1 - y) * Z + z)
    w = xx * 2 + c
    hdev = ((xx * 2 + 1 - yh) * 2 + c, t)

    def ring(d):
        return zdev[d]

    def ring2(d):
        return (dpi, y * Z + lax.rem(z + (2 if d == 0 else Z - 2), Z))

    def tdev(k):
        return (dpi, k)

    def wdev(k):
        return ((k // 2 * 2 + yh) * 2 + lax.rem(k, 2), t)

    def order(j):
        far = 4 - (j + 1) // 2
        return lax.rem(z + (1 - 2 * lax.rem(j + 1, 2)) * far + Z, Z)

    def loop(n, body, first=0):
        def step(i, carry):
            body(i)
            return carry

        lax.fori_loop(first, n, step, 0)

    def both(far, body):
        if far in (0, 4):
            body(lax.rem(z + far, Z))
        else:
            loop(2, lambda i: body(lax.rem(z + far + i * (Z - 2 * far), Z)))

    def local(src, dst, i):
        return pltpu.make_async_copy(src, dst, ld.at[i])

    l_u, l_d = local(u_hbm, uv, 0), local(d_hbm, dv, 1)
    l_h, l_g, l_w = local(h_hbm, hv, 2), local(gain_hbm, gv, 3), local(w_hbm, wv, 4)

    def aload(j):
        k = order(j)
        return pltpu.make_async_copy(a_hbm.at[:, k], av.at[:, k], ls.at[j])


    def xload(j):
        k = order(j)
        return pltpu.make_async_copy(x_hbm.at[:, k], xv.at[:, k], xs.at[j])

    barrier = pltpu.get_barrier_semaphore()

    def hello(dev):
        pl.semaphore_signal(barrier, inc=1, device_id=dev, device_id_type=MESH)

    hello(hdev)
    loop(T - 1, lambda i: hello(tdev(lax.rem(t + 1 + i, T))))
    l_u.start()
    loop(Z, lambda j: aload(j).start())
    l_d.start()
    loop(E - 1, lambda i: hello(wdev(lax.rem(w + 1 + i, E))))
    loop(Z, lambda j: xload(j).start())
    l_h.start()
    l_g.start()
    l_w.start()

    b_rs = ShortRingReduce(lambda k, h: bm.at[k, h], br, sent.at[0], ring_r.at[0], z, ring, ring2)
    b_ag = PairRingGather(bag, sent.at[1], sent.at[27], ring_r.at[1], z, ring)
    p_rs = ShortRingReduce(lambda k, h: pm.at[k, h], pr, sent.at[2], ring_r.at[2], z, ring, ring2)
    p_ag = RingGather(pag, sent.at[3], ring_r.at[3], z, ring, ring2)
    o_rs = RingReduce(lambda k, h: om.at[y * Z + k, h], orr, sent.at[4], ring_r.at[4], z, ring)

    def p_y(j):
        k = order(j)
        return rc(pt.at[k], py.at[k], sent.at[5], py_r.at[j], ydev)

    def o_y(j):
        k = order(j)
        return rc(om.at[(1 - y) * Z + k], oy.at[k], sent.at[6], oy_r.at[j], ydev)

    b_y = rc(bag.at[z, 0], bag.at[z, 1], sent.at[7], y_r.at[0], ydev)

    def b_far(far):
        k = lax.rem(z + far, Z)
        return rc(bag.at[k, 0], bag.at[k, 1], sent.at[25 + far], y_r.at[far - 1], ydev)

    q0_y = rc(q0.at[1], q0y, sent.at[8], y_r.at[1], ydev)

    def p_add(j):
        p_y(j).wait_recv()
        k = order(j)
        pm[k] += py[k]

    def o_add(j):
        o_y(j).wait_recv()
        k = order(j)
        om[y * Z + k] += oy[k]

    def t_copy(n, ref, k):
        return rc(ref, ref, sent.at[9 + n], t_r.at[n], tdev(k))

    def t_send(n, ref):
        loop(T - 1, lambda i: t_copy(n, ref, lax.rem(t + 1 + i, T)).start())

    def t_all(n, some):
        return t_copy(n, some, lax.rem(t + 1, T))

    def z_copy(n, src, dst, k, side=0):
        return rc(src, dst, sent.at[11 + n], z_r.at[n], tdev((y + side - 2 * y * side) * Z + k))

    def z_others(body):
        loop(Z - 1, lambda i: body(lax.rem(z + 1 + i, Z)))

    def z_gather(n, arr):
        z_others(lambda k: z_copy(n, arr.at[z], arr.at[z], k).start())

    def z_all(n, some, side=0):
        return z_copy(n, some, some, lax.rem(z + 1, Z), side)

    def w_copy(n, src, dst, k):
        return rc(src, dst, sent.at[16 + n], w_r.at[n], wdev(k))

    def w_others(body):
        loop(E - 1, lambda i: body(lax.rem(w + 1 + i, E)))

    def w_all(n, some):
        return w_copy(n, some, some, lax.rem(w + 1, E))

    def h_copy(n, src, dst):
        return rc(src, dst, sent.at[21 + n], h_r.at[n], hdev)

    l_u.wait()
    ub[...] = uv[...].astype(BF16)
    blank = jnp.zeros((64, 128), BF16)

    def back(j):
        aload(j).wait()
        k = order(j)
        u1 = jnp.concatenate([ub[...], blank], axis=0)
        u2 = jnp.concatenate([blank, ub[...]], axis=0)
        v = dot_nt(av[0, k], u1) + dot_nt(av[1, k], u2)
        bm[k] = v.reshape(2, CH // 2, 128)

    back(0)
    pl.semaphore_wait(barrier, T - 1 + E - 1 + 1)
    for d in range(2):
        b_rs.antipode(d).start()
    loop(3, back, 1)
    b_rs.begin(True)
    b_rs.begin(False)

    l_d.wait()
    dd = dv[...]
    db[...] = jnp.where(y == 0, dd, swap(dd)).astype(BF16)

    def project(j):
        k = order(j)
        xload(j).wait()
        pa = dot(xv[0, k], db[...])
        pb = dot(xv[1, k], db[...])
        low = low_lanes(CH)
        pm[k] = jnp.where(low, pa, swap(pb)).reshape(2, CH // 2, 128)
        pt[k] = jnp.where(low, swap(pa), pb).reshape(2, CH // 2, 128)

    def project_send(j):
        project(j)
        p_y(j).start()

    loop(4, project_send)
    loop(Z, back, 3)

    l_h.wait()
    l_g.wait()
    hf = hv[...].astype(F32)
    sq = jnp.sum(hf * hf, axis=1, keepdims=True)
    sq = jnp.transpose(jnp.broadcast_to(sq, (256, 128)))
    rows[t, 0:1] = sq[0:1, 0:128]
    rows[t, 1:2] = sq[0:1, 128:256]
    t_send(0, rows.at[t])

    loop(5, project_send, 4)
    b_rs.step(1)
    loop(6, project_send, 5)
    loop(8, project, 6)
    b_rs.step(2)
    p_add(0)
    p_add(1)
    p_add(2)
    for d in range(2):
        p_rs.antipode(d).start()
    p_rs.begin(True)
    b_rs.step(3)
    for h in range(2):
        bag[z, 0, h * 96 : (h + 1) * 96] = b_rs.result(h)
    b_ag.begin(0)
    b_y.start()
    loop(8, lambda j: p_y(j).start(), 6)
    p_rs.begin(False)

    def grad(p, k):
        cot = (bag[k, p] * delta_multiplier).astype(BF16)
        v = dot_tn(cot[:, :64], xv[0, k]) + dot_tn(cot[:, 64:], xv[1, k])
        gt[p] += v.reshape(8, 8, 1024)

    gt[...] = jnp.zeros_like(gt)
    both(0, lambda k: grad(0, k))

    t_all(0, rows.at[0:15]).wait_recv()
    mean = jnp.sum(rows[...], axis=0) / EMBED_DIMENSION
    scale = lax.rsqrt(mean + 1e-05)
    for i in range(2):
        half = slice(i * 128, (i + 1) * 128)
        col = jnp.transpose(jnp.broadcast_to(scale[i : i + 1], (128, 128)))
        for n in range(8):
            sl = slice(n * 128, (n + 1) * 128)
            normed[half, sl] = (hv[half, sl].astype(F32) * col * gv[:, sl]).astype(BF16)

    def pack(v):
        return jnp.where(low_lanes(128), v[:128], v[128:]).reshape(8, 16, 128)

    def twice(v, p):
        keep = low_lanes(256) if p == 0 else jnp.logical_not(low_lanes(256))
        v = jnp.where(keep, v, 0.0)
        return v + swap(v)

    def out_pair(i):
        v = dot(normed[...], wv[:, pl.ds(pl.multiple_of(i * 256, 256), 256)])
        om[2 * i] = v[:, :128].reshape(2, 128, 128)
        om[2 * i + 1] = v[:, 128:].reshape(2, 128, 128)

    dhi, dlo = split(jnp.where(y == 0, dv[...], swap(dv[...])))
    v = dot(normed[...], dhi) + dot(normed[...], dlo)
    for side in range(2):
        q0[side] = pack(twice(v, side))
    q0_y.start()
    l_w.wait()
    loop(4, lambda i: out_pair((1 - y) * 4 + i))
    loop(2, lambda j: o_y(j).start())
    b_ag.step(0, 1)
    b_y.wait_recv()
    b_ag.begin(1)
    both(1, lambda k: grad(0, k))
    both(0, lambda k: grad(1, k))
    p_add(3)
    p_add(4)
    b_ag.step(0, 2)
    p_rs.step(1)
    both(2, lambda k: grad(0, k))
    b_ag.step(1, 1)
    loop(4, lambda i: out_pair(y * 4 + i))
    p_add(5)
    p_add(6)
    b_ag.step(0, 3)
    b_far(3).start()
    b_far(5).start()
    p_rs.step(2)
    both(3, lambda k: grad(0, k))
    both(1, lambda k: grad(1, k))
    b_ag.step(0, 4)
    b_far(4).start()
    loop(4, lambda j: o_y(j).start(), 2)
    both(4, lambda k: grad(0, k))

    def g_reduce(p):
        gr[p, w] = gt[p, w]
        w_others(lambda k: w_copy(p, gt.at[p, k], gr.at[p, w], k).start())

    def g_cross(p):
        w_all(p, gr.at[p, 0:7]).wait_recv()
        gh[p, 0] = jnp.sum(gr[p], axis=0)
        h_copy(p, gh.at[p, 0], gh.at[p, 1]).start()

    def g_gather(p):
        h_copy(p, gh.at[p, 0], gh.at[p, 1]).wait_recv()
        gf[p, w] = gh[p, 0] + gh[p, 1]
        w_others(lambda k: w_copy(2 + p, gf.at[p, w], gf.at[p, w], k).start())

    def g_all(p):
        return w_all(2 + p, gf.at[p, 0:7])

    def up_grad(k):
        pc = (pag[k].reshape(CH, 128) * delta_multiplier).astype(BF16)
        va = dot_tn(pc, av[0, k])
        vb = dot_tn(pc, av[1, k])
        gu[...] += (va[:64] + vb[64:]).reshape(8, 8, 128)

    def q_of(p):
        ghi, glo = split(gf[p].reshape(64, 1024))
        v = dot_nt(normed[...], jnp.concatenate([ghi, glo], axis=0))
        qg[p] = pack(v + swap(v))

    g_reduce(0)
    gu[...] = jnp.zeros_like(gu)
    p_add(7)
    p_rs.step(3)
    for h in range(2):
        pag[z, h] = p_rs.result(h)
    p_ag.begin()
    o_add(0)
    o_rs.begin(1)
    b_ag.step(1, 2)
    both(2, lambda k: grad(1, k))
    b_far(3).wait_recv()
    b_far(5).wait_recv()
    both(3, lambda k: grad(1, k))
    b_far(4).wait_recv()
    both(4, lambda k: grad(1, k))
    g_reduce(1)
    p_ag.step(1)
    g_cross(0)
    loop(5, lambda j: o_y(j).start(), 4)
    both(0, up_grad)
    both(1, up_grad)
    o_add(1)
    o_add(2)
    o_rs.begin(2)
    p_ag.step(2)
    g_cross(1)
    loop(6, lambda j: o_y(j).start(), 5)
    both(2, up_grad)
    g_gather(0)
    g_gather(1)
    loop(7, lambda j: o_y(j).start(), 6)
    o_rs.step(1)
    p_ag.step(3)
    both(3, up_grad)
    both(4, up_grad)
    gur[w] = gu[...]
    w_others(lambda k: w_copy(4, gur.at[w], gur.at[w], k).start())
    loop(8, lambda j: o_y(j).start(), 7)
    q0_y.wait_recv()
    q0[0] += q0y[...]
    q0r[z] = q0[0, z]
    z_others(lambda k: z_copy(0, q0.at[0, k], q0r.at[z], k).start())
    g_all(0).wait_recv()
    q_of(0)
    qgr[0, z] = qg[0, z]
    z_others(lambda k: z_copy(3, qg.at[0, k], qgr.at[0, z], k).start())
    o_add(3)
    o_add(4)
    o_rs.step(2)
    g_all(1).wait_recv()
    q_of(1)
    loop(Z, lambda i: z_copy(4, qg.at[1, lax.rem(z + i, Z)], qgr.at[1, z], lax.rem(z + i, Z), 1).start())
    w_all(4, gur.at[0:7]).wait_recv()
    guh[0] = jnp.sum(gur[...], axis=0)
    gu_h = h_copy(2, guh.at[0], guh.at[1])
    gu_h.start()
    g2 = jnp.sum(gf[...] * gf[...], axis=(0, 1))
    tile = g2[:, 0:128]
    for i in range(1, 8):
        tile = tile + g2[:, i * 128 : (i + 1) * 128]
    z_all(0, q0r.at[0:7]).wait_recv()
    q0a[z] = jnp.sum(q0r[...], axis=0)
    z_gather(1, q0a)
    o_add(5)
    o_add(6)
    o_rs.step(3)
    gu_h.wait_recv()
    guf[...] = guh[0] + guh[1]
    norms[t] = jnp.sum(tile + jnp.sum(guf[...] * guf[...], axis=0), axis=0, keepdims=True)
    t_send(1, norms.at[t])
    z_all(3, qgr.at[0, 0:7]).wait_recv()
    z_all(4, qgr.at[1], 1).wait_recv()
    qga[z] = jnp.sum(qgr[0], axis=0) + jnp.sum(qgr[1], axis=0)
    z_gather(2, qga)
    o_add(7)
    o_rs.step(4)
    for h in range(2):
        base[h] = o_rs.result(h)
    t_all(1, norms.at[0:15]).wait_recv()
    total = jnp.sum(jnp.sum(norms[...], axis=0), keepdims=True)
    factor = jnp.minimum(1.0, clip_limit / (jnp.sqrt(total) + 1e-06))
    up = uv[...] - learning_rate * factor * guf[...].reshape(64, 128)
    zero = jnp.zeros_like(up)
    z_all(1, q0a.at[0:7]).wait_recv()
    z_all(2, qga.at[0:7]).wait_recv()
    q = q0a[...].reshape(128, 128) - learning_rate * factor * qga[...].reshape(128, 128)
    for h in range(2):
        wide = jnp.concatenate([up, zero] if h == 0 else [zero, up], axis=0)
        v = jnp.dot(q, wide, precision=lax.Precision.HIGHEST, preferred_element_type=F32)
        o_ref[:, h * 128 : (h + 1) * 128] = jnp.transpose(base[h] + delta_multiplier * v)

    for exchange in (b_rs, b_ag, p_rs, p_ag, o_rs):
        exchange.drain()
    rc(py, py, sent.at[5], py_r.at[0], ydev).wait_send()
    rc(oy, oy, sent.at[6], oy_r.at[0], ydev).wait_send()
    b_y.wait_send()
    for far in (3, 4, 5):
        b_far(far).wait_send()
    q0_y.wait_send()
    z_all(0, q0r.at[0:7]).wait_send()
    t_all(0, rows.at[0:15]).wait_send()
    t_all(1, norms.at[0:15]).wait_send()
    z_all(1, q0a.at[0:7]).wait_send()
    z_all(2, qga.at[0:7]).wait_send()
    z_all(3, qgr.at[0, 0:7]).wait_send()
    z_all(4, qgr.at[1], 1).wait_send()
    for p in range(2):
        w_all(p, gr.at[p, 0:7]).wait_send()
        g_all(p).wait_send()
        h_copy(p, gh.at[p, 0], gh.at[p, 1]).wait_send()
    w_all(4, gur.at[0:7]).wait_send()
    gu_h.wait_send()


def shards(x, a, w, d, u, hidden, gain):
    V = pltpu.VMEM
    dma = pltpu.SemaphoreType.DMA
    part = (8, 2, 96, 128)
    scratch = [
        V((2, 8, 192, 1024), BF16), V((2, 8, 192, 128), BF16), V((1024, 2048), BF16), V((1024, 128), F32),
        V((64, 128), F32), V((256, 1024), BF16), V((1, 1024), F32), V((1024, 128), BF16), V((64, 128), BF16),
        V(part, F32), V((14, 96, 128), F32), V((8, 2, 192, 128), F32),
        V(part, F32), V(part, F32), V(part, F32), V((14, 96, 128), F32), V(part, F32),
        V((16, 2, 128, 128), F32), V((8, 2, 128, 128), F32), V((14, 128, 128), F32),
        V((2, 8, 8, 1024), F32), V((2, 8, 8, 1024), F32), V((2, 2, 8, 1024), F32), V((2, 8, 8, 1024), F32),
        V((8, 8, 128), F32), V((8, 8, 8, 128), F32), V((2, 8, 8, 128), F32), V((8, 8, 128), F32),
        V((16, 2, 128), F32), V((16, 1, 128), F32), V((256, 1024), BF16), V((2, 128, 128), F32),
        V((2, 8, 16, 128), F32), V((8, 16, 128), F32), V((8, 16, 128), F32), V((8, 16, 128), F32),
        V((2, 8, 16, 128), F32), V((2, 8, 16, 128), F32), V((8, 16, 128), F32),
        dma((5,)), dma((8,)), dma((8,)), dma((5, 14)), dma((8,)), dma((8,)), dma((5,)),
        dma((2,)), dma((5,)), dma((5,)), dma((3,)), dma((31,)),
    ]
    return pl.pallas_call(
        kernel,
        out_shape=jax.ShapeDtypeStruct((128, 256), F32),
        in_specs=[pl.BlockSpec(memory_space=pl.ANY)] * 7,
        out_specs=pl.BlockSpec(memory_space=pltpu.VMEM),
        scratch_shapes=scratch,
        compiler_params=pltpu.CompilerParams(
            collective_id=0, has_side_effects=True, vmem_limit_bytes=56 << 20
        ),
    )(x.reshape(2, 8, CH, 1024), a.reshape(2, 8, CH, 128), w, d, u, hidden, gain.reshape(1, 1024))


def solution(mesh):
    placed = (
        P("dp", "tensor"),
        P("dp", "tensor"),
        P("tensor", None),
        P("tensor", None),
        P(None, "tensor"),
        P("dp", "tensor"),
        P("tensor"),
    )
    return jax.shard_map(
        shards, mesh=mesh, in_specs=placed, out_specs=P("tensor", "dp"), check_vma=False
    )
```

time: 84.9 us -> 81.4 us (0.959)
  the two profiles are of different devices: /device:TPU:1 before, /device:TPU:10 now
where the time goes in v3:
time: 81.4 us; the launch traced here: 81.3 us
  Pallas kernels  79.7 us (98%)
  local copies, waits for them, and re-layouts  1.57 us (2%)
    pallas_call x1, Pallas kernels, shards(): pl.pallas_call(kernel, out_shape=jax.ShapeDtypeStruct((128, 256), F32), i...  79.7 us

profile of v3, /device:TPU:10, one launch (start us, length us, event | category | flops | bytes accessed | tf_op | source)
XLA Modules:
  0.0 81.3 jit_solution(13716438042645606525)
XLA Ops:
  0.0 79.7 %shard_map.73 = f32[128,256]{1,0:T(8,128)} custom-call(bf16[2,8,192,1024]{3,2,1,0:T(8,128)(2,1)} %bitcast.3, bf16[2,8,192,128]{3,2,1,0:T(8,128)(2,1)} %bitcast.4, bf16[1024,2048]{1,0:T(8,128)(2,1)} %w_hbm.1, f32[1024,128]{1,0:T(8,128)} %d_hbm.1, f32[64,128]{1,0:T(8,128)} %u_hbm.1, bf16[256,1024]{1,0:T(8,128)(2,1)} %h_hbm.1, f32[1,1024]{1,0:T(1,128)} %bitcast.5), custom_call_target="tpu_custom_call" | custom-call | tf_op jit(solution)/shard_map/pallas_call | solution.py:632
  79.7 1.6 %copy.9 = f32[128,256]{1,0:T(8,128)} copy(f32[128,256]{1,0:T(8,128)} %shard_map.73) | data formatting | bytes 262144

commit v4 on v3

--- a/solution.py
+++ b/solution.py
@@ -240,6 +240,9 @@
         else:
             loop(2, lambda i: body(lax.rem(z + far + i * (Z - 2 * far), Z)))
 
+    def on(core, body):
+        pl.when(c == core)(body)
+
     def local(src, dst, i):
         return pltpu.make_async_copy(src, dst, ld.at[i])
 
@@ -273,7 +276,7 @@
 
     b_rs = ShortRingReduce(lambda k, h: bm.at[k, h], br, sent.at[0], ring_r.at[0], z, ring, ring2)
     b_ag = PairRingGather(bag, sent.at[1], sent.at[27], ring_r.at[1], z, ring)
-    p_rs = ShortRingReduce(lambda k, h: pm.at[k, h], pr, sent.at[2], ring_r.at[2], z, ring, ring2)
+    p_rs = RingReduce(lambda k, h: pm.at[k, h], pr, sent.at[2], ring_r.at[2], z, ring)
     p_ag = RingGather(pag, sent.at[3], ring_r.at[3], z, ring, ring2)
     o_rs = RingReduce(lambda k, h: om.at[y * Z + k, h], orr, sent.at[4], ring_r.at[4], z, ring)
 
@@ -389,20 +392,19 @@
     b_rs.step(1)
     loop(6, project_send, 5)
     loop(8, project, 6)
+    p_add(0)
+    p_rs.begin(1)
     b_rs.step(2)
-    p_add(0)
     p_add(1)
     p_add(2)
-    for d in range(2):
-        p_rs.antipode(d).start()
-    p_rs.begin(True)
+    p_rs.begin(2)
     b_rs.step(3)
     for h in range(2):
         bag[z, 0, h * 96 : (h + 1) * 96] = b_rs.result(h)
     b_ag.begin(0)
     b_y.start()
     loop(8, lambda j: p_y(j).start(), 6)
-    p_rs.begin(False)
+    p_rs.step(1)
 
     def grad(p, k):
         cot = (bag[k, p] * delta_multiplier).astype(BF16)
@@ -451,7 +453,7 @@
     p_add(3)
     p_add(4)
     b_ag.step(0, 2)
-    p_rs.step(1)
+    p_rs.step(2)
     both(2, lambda k: grad(0, k))
     b_ag.step(1, 1)
     loop(4, lambda i: out_pair(y * 4 + i))
@@ -460,12 +462,12 @@
     b_ag.step(0, 3)
     b_far(3).start()
     b_far(5).start()
-    p_rs.step(2)
+    p_rs.step(3)
     both(3, lambda k: grad(0, k))
     both(1, lambda k: grad(1, k))
     b_ag.step(0, 4)
     b_far(4).start()
-    loop(4, lambda j: o_y(j).start(), 2)
+    loop(3, lambda j: o_y(j).start(), 2)
     both(4, lambda k: grad(0, k))
 
     def g_reduce(p):
@@ -499,7 +501,7 @@
     g_reduce(0)
     gu[...] = jnp.zeros_like(gu)
     p_add(7)
-    p_rs.step(3)
+    p_rs.step(4)
     for h in range(2):
         pag[z, h] = p_rs.result(h)
     p_ag.begin()
@@ -515,40 +517,48 @@
     g_reduce(1)
     p_ag.step(1)
     g_cross(0)
-    loop(5, lambda j: o_y(j).start(), 4)
+    loop(4, lambda j: o_y(j).start(), 3)
     both(0, up_grad)
     both(1, up_grad)
     o_add(1)
     o_add(2)
     o_rs.begin(2)
-    p_ag.step(2)
+    o_rs.step(1)
+    on(1, lambda: p_ag.step(2))
     g_cross(1)
-    loop(6, lambda j: o_y(j).start(), 5)
+    g_gather(0)
+    loop(6, lambda j: o_y(j).start(), 4)
+    on(0, lambda: p_ag.step(2))
     both(2, up_grad)
-    g_gather(0)
+    q0_y.wait_recv()
+    q0[0] += q0y[...]
+    q0r[z] = q0[0, z]
+    z_others(lambda k: z_copy(0, q0.at[0, k], q0r.at[z], k).start())
     g_gather(1)
     loop(7, lambda j: o_y(j).start(), 6)
-    o_rs.step(1)
+    o_add(3)
+    o_add(4)
+    on(0, lambda: o_rs.step(2))
     p_ag.step(3)
+    on(1, lambda: o_rs.step(2))
     both(3, up_grad)
     both(4, up_grad)
     gur[w] = gu[...]
     w_others(lambda k: w_copy(4, gur.at[w], gur.at[w], k).start())
     loop(8, lambda j: o_y(j).start(), 7)
-    q0_y.wait_recv()
-    q0[0] += q0y[...]
-    q0r[z] = q0[0, z]
-    z_others(lambda k: z_copy(0, q0.at[0, k], q0r.at[z], k).start())
+    z_all(0, q0r.at[0:7]).wait_recv()
+    q0a[z] = jnp.sum(q0r[...], axis=0)
+    z_gather(1, q0a)
     g_all(0).wait_recv()
     q_of(0)
     qgr[0, z] = qg[0, z]
     z_others(lambda k: z_copy(3, qg.at[0, k], qgr.at[0, z], k).start())
-    o_add(3)
-    o_add(4)
-    o_rs.step(2)
     g_all(1).wait_recv()
     q_of(1)
     loop(Z, lambda i: z_copy(4, qg.at[1, lax.rem(z + i, Z)], qgr.at[1, z], lax.rem(z + i, Z), 1).start())
+    o_add(5)
+    o_add(6)
+    o_rs.step(3)
     w_all(4, gur.at[0:7]).wait_recv()
     guh[0] = jnp.sum(gur[...], axis=0)
     gu_h = h_copy(2, guh.at[0], guh.at[1])
@@ -557,12 +567,6 @@
     tile = g2[:, 0:128]
     for i in range(1, 8):
         tile = tile + g2[:, i * 128 : (i + 1) * 128]
-    z_all(0, q0r.at[0:7]).wait_recv()
-    q0a[z] = jnp.sum(q0r[...], axis=0)
-    z_gather(1, q0a)
-    o_add(5)
-    o_add(6)
-    o_rs.step(3)
     gu_h.wait_recv()
     guf[...] = guh[0] + guh[1]
     norms[t] = jnp.sum(tile + jnp.sum(guf[...] * guf[...], axis=0), axis=0, keepdims=True)

time: 81.4 us -> 79.8 us (0.980)
  the two profiles are of different devices: /device:TPU:10 before, /device:TPU:1 now
where the time goes in v4:
time: 79.8 us; the launch traced here: 79.7 us
  Pallas kernels  78.1 us (98%)
  local copies, waits for them, and re-layouts  1.57 us (2%)
    pallas_call x1, Pallas kernels, shards(): pl.pallas_call(kernel, out_shape=jax.ShapeDtypeStruct((128, 256), F32), i...  78.1 us

profile of v4, /device:TPU:1, one launch (start us, length us, event | category | flops | bytes accessed | tf_op | source)
XLA Modules:
  0.0 79.7 jit_solution(5783885328380005231)
XLA Ops:
  0.0 78.1 %shard_map.73 = f32[128,256]{1,0:T(8,128)} custom-call(bf16[2,8,192,1024]{3,2,1,0:T(8,128)(2,1)} %bitcast.3, bf16[2,8,192,128]{3,2,1,0:T(8,128)(2,1)} %bitcast.4, bf16[1024,2048]{1,0:T(8,128)(2,1)} %w_hbm.1, f32[1024,128]{1,0:T(8,128)} %d_hbm.1, f32[64,128]{1,0:T(8,128)} %u_hbm.1, bf16[256,1024]{1,0:T(8,128)(2,1)} %h_hbm.1, f32[1,1024]{1,0:T(1,128)} %bitcast.5), custom_call_target="tpu_custom_call" | custom-call | tf_op jit(solution)/shard_map/pallas_call | solution.py:636
  78.2 1.6 %copy.9 = f32[128,256]{1,0:T(8,128)} copy(f32[128,256]{1,0:T(8,128)} %shard_map.73) | data formatting | bytes 262144

commit v5 on v4

--- a/solution.py
+++ b/solution.py
@@ -522,13 +522,18 @@
     both(1, up_grad)
     o_add(1)
     o_add(2)
-    o_rs.begin(2)
-    o_rs.step(1)
+
+    def more():
+        o_rs.begin(2)
+        o_rs.step(1)
+
+    on(1, more)
     on(1, lambda: p_ag.step(2))
     g_cross(1)
     g_gather(0)
     loop(6, lambda j: o_y(j).start(), 4)
     on(0, lambda: p_ag.step(2))
+    on(0, more)
     both(2, up_grad)
     q0_y.wait_recv()
     q0[0] += q0y[...]
@@ -536,33 +541,38 @@
     z_others(lambda k: z_copy(0, q0.at[0, k], q0r.at[z], k).start())
     g_gather(1)
     loop(7, lambda j: o_y(j).start(), 6)
+
+    def q_own():
+        g_all(0).wait_recv()
+        q_of(0)
+        qgr[0, z] = qg[0, z]
+        z_others(lambda k: z_copy(3, qg.at[0, k], qgr.at[0, z], k).start())
+
+    on(0, q_own)
+    p_ag.step(3)
     o_add(3)
     o_add(4)
-    on(0, lambda: o_rs.step(2))
-    p_ag.step(3)
     on(1, lambda: o_rs.step(2))
     both(3, up_grad)
     both(4, up_grad)
     gur[w] = gu[...]
     w_others(lambda k: w_copy(4, gur.at[w], gur.at[w], k).start())
-    loop(8, lambda j: o_y(j).start(), 7)
+    on(0, lambda: o_rs.step(2))
+    on(1, q_own)
+    g_all(1).wait_recv()
+    q_of(1)
+    loop(Z, lambda i: z_copy(4, qg.at[1, lax.rem(z + i, Z)], qgr.at[1, z], lax.rem(z + i, Z), 1).start())
     z_all(0, q0r.at[0:7]).wait_recv()
     q0a[z] = jnp.sum(q0r[...], axis=0)
     z_gather(1, q0a)
-    g_all(0).wait_recv()
-    q_of(0)
-    qgr[0, z] = qg[0, z]
-    z_others(lambda k: z_copy(3, qg.at[0, k], qgr.at[0, z], k).start())
-    g_all(1).wait_recv()
-    q_of(1)
-    loop(Z, lambda i: z_copy(4, qg.at[1, lax.rem(z + i, Z)], qgr.at[1, z], lax.rem(z + i, Z), 1).start())
-    o_add(5)
-    o_add(6)
-    o_rs.step(3)
     w_all(4, gur.at[0:7]).wait_recv()
     guh[0] = jnp.sum(gur[...], axis=0)
     gu_h = h_copy(2, guh.at[0], guh.at[1])
     gu_h.start()
+    o_y(7).start()
+    o_add(5)
+    o_add(6)
+    o_rs.step(3)
     g2 = jnp.sum(gf[...] * gf[...], axis=(0, 1))
     tile = g2[:, 0:128]
     for i in range(1, 8):

time: 79.8 us -> 78.1 us (0.979)
  Pallas kernels: 78.1 us -> 76.4 us
    pallas_call x1, Pallas kernels: 78.1 us -> 76.4 us  [shards(): pl.pallas_call(kernel, out_shape=jax.ShapeDtypeStruct((128, 256), F32), i...]
where the time goes in v5:
time: 78.1 us; the launch traced here: 78 us
  Pallas kernels  76.4 us (98%)
  local copies, waits for them, and re-layouts  1.57 us (2%)
    pallas_call x1, Pallas kernels, shards(): pl.pallas_call(kernel, out_shape=jax.ShapeDtypeStruct((128, 256), F32), i...  76.4 us
    unnamed x1, local copies, waits for them, and re-layouts  1.57 us

profile of v5, /device:TPU:1, one launch (start us, length us, event | category | flops | bytes accessed | tf_op | source)
XLA Modules:
  0.0 78.0 jit_solution(10883112596224969206)
XLA Ops:
  0.0 76.4 %shard_map.73 = f32[128,256]{1,0:T(8,128)} custom-call(bf16[2,8,192,1024]{3,2,1,0:T(8,128)(2,1)} %bitcast.3, bf16[2,8,192,128]{3,2,1,0:T(8,128)(2,1)} %bitcast.4, bf16[1024,2048]{1,0:T(8,128)(2,1)} %w_hbm.1, f32[1024,128]{1,0:T(8,128)} %d_hbm.1, f32[64,128]{1,0:T(8,128)} %u_hbm.1, bf16[256,1024]{1,0:T(8,128)(2,1)} %h_hbm.1, f32[1,1024]{1,0:T(1,128)} %bitcast.5), custom_call_target="tpu_custom_call" | custom-call | tf_op jit(solution)/shard_map/pallas_call | solution.py:646
  76.4 1.6 %copy.9 = f32[128,256]{1,0:T(8,128)} copy(f32[128,256]{1,0:T(8,128)} %shard_map.73) | data formatting | bytes 262144

commit v6 on v5

--- a/solution.py
+++ b/solution.py
@@ -119,9 +119,10 @@
                     self.copy(d, p, 4).start()
                 if s < 3:
                     self.copy(d, p, s + 1).start()
-        if s == 3:
-            for d in range(2):
-                self.copy(d, d, 4).wait_recv()
+
+    def last(self):
+        for d in range(2):
+            self.copy(d, d, 4).wait_recv()
 
     def drain(self):
         all_sent = self.arr.at[0:7]
@@ -251,7 +252,7 @@
 
     def aload(j):
         k = order(j)
-        return pltpu.make_async_copy(a_hbm.at[:, k], av.at[:, k], ls.at[j])
+        return pltpu.make_async_copy(a_hbm.at[:, k], av.at[:, k], ls.at[jnp.minimum(j, 1)])
 
 
     def xload(j):
@@ -344,14 +345,15 @@
     blank = jnp.zeros((64, 128), BF16)
 
     def back(j):
-        aload(j).wait()
         k = order(j)
         u1 = jnp.concatenate([ub[...], blank], axis=0)
         u2 = jnp.concatenate([blank, ub[...]], axis=0)
         v = dot_nt(av[0, k], u1) + dot_nt(av[1, k], u2)
         bm[k] = v.reshape(2, CH // 2, 128)
 
+    aload(0).wait()
     back(0)
+    pltpu.make_async_copy(a_hbm.at[:, 0:7], av.at[:, 0:7], ls.at[1]).wait()
     pl.semaphore_wait(barrier, T - 1 + E - 1 + 1)
     for d in range(2):
         b_rs.antipode(d).start()
@@ -550,11 +552,12 @@
 
     on(0, q_own)
     p_ag.step(3)
+    both(3, up_grad)
+    p_ag.last()
+    both(4, up_grad)
     o_add(3)
     o_add(4)
     on(1, lambda: o_rs.step(2))
-    both(3, up_grad)
-    both(4, up_grad)
     gur[w] = gu[...]
     w_others(lambda k: w_copy(4, gur.at[w], gur.at[w], k).start())
     on(0, lambda: o_rs.step(2))
@@ -562,14 +565,14 @@
     g_all(1).wait_recv()
     q_of(1)
     loop(Z, lambda i: z_copy(4, qg.at[1, lax.rem(z + i, Z)], qgr.at[1, z], lax.rem(z + i, Z), 1).start())
-    z_all(0, q0r.at[0:7]).wait_recv()
-    q0a[z] = jnp.sum(q0r[...], axis=0)
-    z_gather(1, q0a)
     w_all(4, gur.at[0:7]).wait_recv()
     guh[0] = jnp.sum(gur[...], axis=0)
     gu_h = h_copy(2, guh.at[0], guh.at[1])
     gu_h.start()
     o_y(7).start()
+    z_all(0, q0r.at[0:7]).wait_recv()
+    q0a[z] = jnp.sum(q0r[...], axis=0)
+    z_gather(1, q0a)
     o_add(5)
     o_add(6)
     o_rs.step(3)
@@ -640,7 +643,7 @@
         V((16, 2, 128), F32), V((16, 1, 128), F32), V((256, 1024), BF16), V((2, 128, 128), F32),
         V((2, 8, 16, 128), F32), V((8, 16, 128), F32), V((8, 16, 128), F32), V((8, 16, 128), F32),
         V((2, 8, 16, 128), F32), V((2, 8, 16, 128), F32), V((8, 16, 128), F32),
-        dma((5,)), dma((8,)), dma((8,)), dma((5, 14)), dma((8,)), dma((8,)), dma((5,)),
+        dma((5,)), dma((2,)), dma((8,)), dma((5, 14)), dma((8,)), dma((8,)), dma((5,)),
         dma((2,)), dma((5,)), dma((5,)), dma((3,)), dma((31,)),
     ]
     return pl.pallas_call(

time: 78.1 us -> 79.1 us (1.013)
  Pallas kernels: 76.4 us -> 77.4 us
    pallas_call x1, Pallas kernels: 76.4 us -> 77.4 us  [shards(): pl.pallas_call(kernel, out_shape=jax.ShapeDtypeStruct((128, 256), F32), i...]
where the time goes in v6:
time: 79.1 us; the launch traced here: 79 us
  Pallas kernels  77.4 us (98%)
  local copies, waits for them, and re-layouts  1.57 us (2%)
    pallas_call x1, Pallas kernels, shards(): pl.pallas_call(kernel, out_shape=jax.ShapeDtypeStruct((128, 256), F32), i...  77.4 us

profile of v6, /device:TPU:1, one launch (start us, length us, event | category | flops | bytes accessed | tf_op | source)
XLA Modules:
  0.0 79.0 jit_solution(4168895759005970667)
XLA Ops:
  0.0 77.4 %shard_map.73 = f32[128,256]{1,0:T(8,128)} custom-call(bf16[2,8,192,1024]{3,2,1,0:T(8,128)(2,1)} %bitcast.3, bf16[2,8,192,128]{3,2,1,0:T(8,128)(2,1)} %bitcast.4, bf16[1024,2048]{1,0:T(8,128)(2,1)} %w_hbm.1, f32[1024,128]{1,0:T(8,128)} %d_hbm.1, f32[64,128]{1,0:T(8,128)} %u_hbm.1, bf16[256,1024]{1,0:T(8,128)(2,1)} %h_hbm.1, f32[1,1024]{1,0:T(1,128)} %bitcast.5), custom_call_target="tpu_custom_call" | custom-call | tf_op jit(solution)/shard_map/pallas_call | solution.py:649
  77.4 1.6 %copy.9 = f32[128,256]{1,0:T(8,128)} copy(f32[128,256]{1,0:T(8,128)} %shard_map.73) | data formatting | bytes 262144
